TPU v7x, 32 devices: a whole 2x2x4 slice. The times are simulated.
32 devices in a mesh: parts: 2 (over y), node: 4 (over z), local: 4 (over x, core).
Axes of the slice: x: 2, y: 2, z: 4, core: 2. Of those that a mesh axis runs over, the one named last changes fastest.
Arguments:
- tokens: bfloat16 [256, 7168], P(('parts', 'node', 'local')), parts along dimension 0, may hold values from -6 to 6
- expert_ids: int32 [256, 8], P(('parts', 'node', 'local')), parts along dimension 0, may hold values from 0 to 15, as said below
- gate_weights: bfloat16 [256, 8], P(('parts', 'node', 'local')), parts along dimension 0, may hold values from 0.099609375 to 1
- w_gate_up: bfloat16 [16, 7168, 2048], P(('node', 'local')), may hold values from -0.0625 to 0.0625
- gate_up_scales: float32 [16, 56, 16], P(('node', 'local')), may hold values from 0.5 to 2
- w_down: bfloat16 [16, 1024, 7168], P(('node', 'local')), may hold values from -0.1875 to 0.1875
- down_scales: float32 [16, 8, 56], P(('node', 'local')), may hold values from 0.5 to 2
Outputs:
- combined: bfloat16 [256, 7168], P(('parts', 'node', 'local')), parts along dimension 0
There are 2 independent parts, one for each index of `parts`. A program takes and returns all parts, laid end to end along the dimension named above; an argument that names none is the same for every part. Nothing has to cross between parts.
Inputs may be any that keep to these rules, and one draw needn't show every extreme that they name: `expert_ids`: each row names 8 different experts, 2 in each of 4 different node groups; expert e belongs to node group e // 4. Among the 8 rows of one device no expert is named by more than 4 rows, and one expert is named by exactly 4 rows of every device.
All inputs are finite; a program needn't handle non-finite values.
Results may differ from a plain program's by a relative error of at most 0.011.
Values may be sent and summed in bfloat16 or wider, within the bound.
No kernel may reach another device: no remote copies, remote signals or barrier semaphores. Data moves between devices by JAX's collectives and lax.ppermute only.
A program may use at most 128 MiB of HBM per device.

v0:
```python
import jax
import jax.numpy as jnp
from jax import lax
from jax.sharding import PartitionSpec as P

TOPK = 8
GROUP_LIMIT = 4
EXP_GROUP = 4


def block_project(operand, weights, scales):
    row_total, inner = operand.shape
    out_width = weights.shape[1]
    weight_blocks = weights.reshape(inner // 128, 128, out_width)
    column_scale = jnp.repeat(scales, 128, axis=1)

    def one_block(row_block):
        products = jnp.einsum(
            "mkc,kcn->mkn",
            row_block.reshape(row_block.shape[0], inner // 128, 128),
            weight_blocks,
            preferred_element_type=jnp.float32,
        )
        return jnp.sum(products * column_scale[None], axis=1)

    if row_total % 128 == 0:
        block_rows = 128
    else:
        block_rows = row_total
    mapped = lax.map(one_block, operand.reshape(row_total // block_rows, block_rows, inner))
    return mapped.reshape(row_total, out_width)


def expert_apply(operand, gate_up, gate_up_scale, down, down_scale):
    half_width = down.shape[0]
    hidden_pair = block_project(operand, gate_up, gate_up_scale)
    activation = (jax.nn.silu(hidden_pair[:, :half_width]) * hidden_pair[:, half_width:]).astype(
        jnp.bfloat16
    )
    return block_project(activation, down, down_scale).astype(jnp.bfloat16)


def weighted_sum(pick_float, slot_values, form):
    return jnp.einsum(
        form,
        pick_float,
        slot_values,
        precision=lax.Precision.HIGHEST,
        preferred_element_type=jnp.float32,
    )


def shards(tokens, expert_ids, gate_weights, w_gate_up, gate_up_scales, w_down, down_scales):
    group_count = lax.axis_size("node")
    owner_count = lax.axis_size("local")
    row_count, feat_width = tokens.shape
    member_count = EXP_GROUP
    slice_count = owner_count // member_count
    expert_count = group_count * member_count
    round_len = member_count * GROUP_LIMIT // TOPK
    slot_cap = row_count // round_len
    expert_range = jnp.arange(expert_count, dtype=jnp.int32)
    hit_table = expert_ids[:, :, None] == expert_range[None, None, :]
    gate_full = jnp.sum(
        jnp.where(hit_table, gate_weights.astype(jnp.float32)[:, :, None], jnp.float32(0.0)), axis=1
    )
    routed = jnp.any(hit_table, axis=1)
    position = jnp.cumsum(routed.astype(jnp.int32), axis=0) - 1
    slot_range = jnp.arange(slot_cap, dtype=jnp.int32)
    pick_mask = routed.T[:, None, :] & (position.T[:, None, :] == slot_range[None, :, None])
    pick_table = pick_mask.astype(jnp.bfloat16)
    expert_rows = jnp.einsum(
        "ecr,rd->ecd", pick_table, tokens, preferred_element_type=jnp.float32
    ).astype(jnp.bfloat16)
    send_rows = jnp.repeat(expert_rows, slice_count, axis=0)
    received = lax.all_to_all(send_rows, ("node", "local"), split_axis=0, concat_axis=0, tiled=True)
    full_shape = received.shape
    flattened = received.reshape(-1, feat_width)
    outputs = expert_apply(flattened, w_gate_up[0], gate_up_scales[0], w_down[0], down_scales[0])
    returned = lax.all_to_all(
        outputs.reshape(full_shape), ("node", "local"), split_axis=0, concat_axis=0, tiled=True
    )
    returned = returned.reshape(expert_count, slice_count, slot_cap, feat_width)
    expert_out = jnp.sum(returned.astype(jnp.float32), axis=1)
    pick_float = pick_mask.astype(jnp.float32)
    slot_gate = jnp.sum(pick_float * gate_full.T[:, None, :], axis=2)
    weighted_out = expert_out * slot_gate[:, :, None]
    pick_grouped = pick_float.reshape(group_count, member_count, slot_cap, row_count)
    weighted_grouped = weighted_out.reshape(group_count, member_count, slot_cap, feat_width)
    combined_sum = jnp.zeros((row_count, feat_width), jnp.float32)
    for group_idx in range(group_count):
        partial_sum = weighted_sum(
            pick_grouped[group_idx], weighted_grouped[group_idx], "ecr,ecd->rd"
        ).astype(jnp.bfloat16)
        combined_sum = combined_sum + lax.optimization_barrier(partial_sum).astype(jnp.float32)
    return combined_sum.astype(jnp.bfloat16)


def solution(mesh):
    in_specs = (
        P(("parts", "node", "local"), None),
        P(("parts", "node", "local"), None),
        P(("parts", "node", "local"), None),
        P(("node", "local"), None, None),
        P(("node", "local"), None, None),
        P(("node", "local"), None, None),
        P(("node", "local"), None, None),
    )
    out_specs = P(("parts", "node", "local"), None)
    return jax.shard_map(shards, mesh=mesh, in_specs=in_specs, out_specs=out_specs, check_vma=False)
```

profile of v0, /device:TPU:0, one launch (start us, length us, event | category | flops | bytes accessed | tf_op | source)
XLA Modules:
  0.0 84.9 jit_solution(12151647772845908478)
XLA Ops:
  0.0 0.8 fusion.14
  1.0 0.7 convert_element_type.58
  1.7 0.8 select_reduce_fusion.1
  2.6 0.1 select_reduce_fusion
  2.7 0.4 convolution_convert_fusion
  3.0 1.6 %copy.28 = bf16[16,4,7168]{2,1,0:T(4,128)(2,1)} copy(bf16[16,4,7168]{2,0,1:T(8,128)(2,1)S(1)} %convolution_convert_fusion) | data formatting | bytes 1835008 | tf_op jit(solution)/shard_map/convert_element_type | solution.py:74
  4.7 7.4 %all-to-all-start = ((bf16[16,4,7168]{2,1,0:T(4,128)(2,1)}), bf16[16,4,7168]{2,1,0:T(4,128)(2,1)S(1)}, u32[]{:S(2)}, u32[]{:S(2)}) async-start(bf16[16,4,7168]{2,1,0:T(4,128)(2,1)} %copy.28), calls=%async_computation | async-start | bytes 1835008 | tf_op jit(solution)/shard_map/all_to_all | solution.py:76
  12.0 0.8 copy.30
  12.8 0.8 copy.32
  13.6 0.2 broadcast_in_dim.22
  13.8 0.1 copy.46
  13.9 0.1 broadcast_bitcast_fusion
  14.0 18.8 %all-to-all-done = bf16[16,4,7168]{2,1,0:T(4,128)(2,1)S(1)} async-done(((bf16[16,4,7168]{2,1,0:T(4,128)(2,1)}), bf16[16,4,7168]{2,1,0:T(4,128)(2,1)S(1)}, u32[]{:S(2)}, u32[]{:S(2)}) %all-to-all-start) | async-done | bytes 917536 | tf_op jit(solution)/shard_map/all_to_all | solution.py:76
  32.9 0.3 reshape.51
  33.2 11.9 %multiply_reduce_fusion = f32[64,2048]{1,0:T(8,128)S(1)} fusion(bf16[56,128,2048]{2,1,0:T(8,128)(2,1)} %bitcast.43, f32[56,2048]{1,0:T(8,128)S(1)} %bitcast.45, bf16[64,56,128]{2,1,0:T(8,128)(2,1)S(1)} %reshape.51), kind=kOutput, calls=%fused_computation | convolution fusion | flops 1893597184 | bytes 31260672 | tf_op jit(solution)/shard_map/while/body/eval_jaxpr/mkc,kcn->mkn/dot_general | solution.py:18
  45.1 7.9 %multiply_reduce_fusion.1 = bf16[64,7168]{1,0:T(8,128)(2,1)S(1)} fusion(bf16[8,128,7168]{2,1,0:T(8,128)(2,1)} %bitcast.44, f32[8,7168]{1,0:T(8,128)S(1)} %broadcast_bitcast_fusion, f32[64,2048]{1,0:T(8,128)S(1)} %multiply_reduce_fusion), kind=kOutput, calls=%fused_computation.1 | convolution fusion | flops 946798592 | bytes 16351232 | tf_op jit(solution)/shard_map/while/body/eval_jaxpr/mkc,kcn->mkn/dot_general | solution.py:18
  53.0 0.3 convert_element_type.56
  53.3 28.5 %all_to_all.10 = bf16[16,4,7168]{2,1,0:T(4,128)(2,1)S(1)} all-to-all(bf16[16,4,7168]{2,1,0:T(4,128)(2,1)S(1)} %convert_element_type.56), channel_id=1, replica_groups=mesh['parts'=2,'node'=4,'local'=4] {'node','local'}, dimensions={0} | all-to-all | bytes 1835008 | tf_op jit(solution)/shard_map/all_to_all | solution.py:80
  81.9 0.3 convert_multiply_fusion
  82.2 0.6 fusion.3
  82.7 0.4 fusion.2
  83.2 0.6 fusion.1
  83.8 0.4 fusion
  84.2 0.7 add_convert_fusion
  (8 shorter events, 0.3 us)
Async XLA Ops:
  0.0 2.7 %copy-start = (bf16[8,7168]{1,0:T(8,128)(2,1)S(1)}, bf16[8,7168]{1,0:T(8,128)(2,1)}, u32[]{:S(2)}) copy-start(bf16[8,7168]{1,0:T(8,128)(2,1)} %param.7) | copy-start | bytes 344068
  4.7 28.2 %all-to-all-start = ((bf16[16,4,7168]{2,1,0:T(4,128)(2,1)}), bf16[16,4,7168]{2,1,0:T(4,128)(2,1)S(1)}, u32[]{:S(2)}, u32[]{:S(2)}) async-start(bf16[16,4,7168]{2,1,0:T(4,128)(2,1)} %copy.28), calls=%async_computation | async-start | bytes 1835008 | tf_op jit(solution)/shard_map/all_to_all | solution.py:76
where the time goes:
time: 85.6 us; the launch traced here: 84.9 us
  blocking collectives  28.5 us (33%)
  matrix products  22.1 us (26%)
  waiting for transfers between devices  18.8 us (22%)
  starting transfers between devices  7.36 us (9%)
  local copies, waits for them, and re-layouts  4.53 us (5%)
  other arithmetic  3.42 us (4%)
    all_to_all x1, blocking collectives, shards(): lax.all_to_all(outputs.reshape(full_shape), ('node', 'local'), split_axis...  28.5 us
    dot_general x2, matrix products, one_block(): jnp.einsum('mkc,kcn->mkn', row_block.reshape(row_block.shape[0], inner //...  19.8 us
    all_to_all x1, waiting for transfers between devices, shards(): lax.all_to_all(send_rows, ('node', 'local'), split_axis=0, concat_axis=0,...  18.8 us
    all_to_all x1, starting transfers between devices, shards(): lax.all_to_all(send_rows, ('node', 'local'), split_axis=0, concat_axis=0,...  7.36 us
    dot_general x4, matrix products, weighted_sum(): jnp.einsum(form, pick_float, slot_values, precision=lax.Precision.HIGHEST...  2 us
  transfers between devices with their start and end apart: 1, of which 1 were waited for; matrix products, arithmetic and copies ran while one was open for 2% of the time, Pallas kernels for 0%

commit v1 on v0

v1 whole, which is shorter than its diff:
```python
import functools

import jax
import jax.numpy as jnp
from jax import lax
from jax.experimental import pallas as pl
from jax.experimental.pallas import tpu as pltpu
from jax.sharding import PartitionSpec as P

EXP_GROUP = 4
LANES = 128
BLOCK = 128
VMEM = pl.BlockSpec(memory_space=pltpu.VMEM)
SMEM = pl.BlockSpec(memory_space=pltpu.SMEM)


def pack_kernel(tokens_ref, ids_ref, gates_ref, out_ref):
    rows, width = tokens_ref.shape
    out_ref[:, :width] = tokens_ref[...]
    lane = lax.broadcasted_iota(jnp.int32, (rows, LANES), 1)
    ids = ids_ref[...]
    gates = gates_ref[...].astype(jnp.float32)
    route = jnp.zeros((rows, LANES), jnp.float32)
    for k in range(ids.shape[1]):
        route = route + jnp.where(ids[:, k : k + 1] == lane, gates[:, k : k + 1], 0.0)
    out_ref[:, width:] = route.astype(jnp.bfloat16)


def pack_rows(tokens, ids, gates):
    rows, width = tokens.shape
    return pl.pallas_call(
        pack_kernel,
        out_shape=jax.ShapeDtypeStruct((rows, width + LANES), jnp.bfloat16),
        in_specs=[VMEM, VMEM, VMEM],
        out_specs=VMEM,
    )(tokens, ids, gates)


def tile_of(width, most=512):
    tile = most
    while width % tile:
        tile -= BLOCK
    return tile


def expert_kernel(which_ref, rows_ref, up_ref, up_scale_ref, down_ref, down_scale_ref, out_ref, hidden_ref, act_ref):
    count = rows_ref.shape[0]
    depth, pair = up_ref.shape
    half, width = down_ref.shape
    tile = tile_of(pair)

    @pl.loop(0, pair // tile)
    def _(step):
        cols = pl.ds(pl.multiple_of(step * tile, tile), tile)
        total = jnp.zeros((count, tile), jnp.float32)
        for b in range(depth // BLOCK):
            part = jnp.dot(
                rows_ref[:, b * BLOCK : (b + 1) * BLOCK],
                up_ref[b * BLOCK : (b + 1) * BLOCK, cols],
                preferred_element_type=jnp.float32,
            )
            total = total + part * up_scale_ref[b : b + 1, cols]
        hidden_ref[:, cols] = total

    gate = hidden_ref[:, :half]
    act_ref[...] = (gate / (1.0 + jnp.exp(-gate)) * hidden_ref[:, half:]).astype(jnp.bfloat16)
    route = rows_ref[:, depth:].astype(jnp.float32)
    lane = lax.broadcasted_iota(jnp.int32, route.shape, 1)
    mine = jnp.sum(jnp.where(lane == which_ref[0], route, 0.0), axis=1, keepdims=True)
    tile_out = tile_of(width)

    @pl.loop(0, width // tile_out)
    def _(step):
        cols = pl.ds(pl.multiple_of(step * tile_out, tile_out), tile_out)
        total = jnp.zeros((count, tile_out), jnp.float32)
        for b in range(half // BLOCK):
            part = jnp.dot(
                act_ref[:, b * BLOCK : (b + 1) * BLOCK],
                down_ref[b * BLOCK : (b + 1) * BLOCK, cols],
                preferred_element_type=jnp.float32,
            )
            total = total + part * down_scale_ref[b : b + 1, cols]
        out_ref[:, cols] = jnp.where(mine > 0, total * mine, 0.0).astype(jnp.bfloat16)


def expert_apply(which, rows, up, up_scale, down, down_scale):
    count = rows.shape[0]
    half, width = down.shape
    moved = (up.size + down.size) * 2
    return pl.pallas_call(
        expert_kernel,
        out_shape=jax.ShapeDtypeStruct((count, width), jnp.bfloat16),
        in_specs=[SMEM] + [VMEM] * 5,
        out_specs=VMEM,
        scratch_shapes=[
            pltpu.VMEM((count, 2 * half), jnp.float32),
            pltpu.VMEM((count, half), jnp.bfloat16),
        ],
        compiler_params=pltpu.CompilerParams(vmem_limit_bytes=14 << 20),
        cost_estimate=pl.CostEstimate(
            flops=2 * count * (up.size + down.size), bytes_accessed=moved, transcendentals=count * half
        ),
    )(which, rows, up, up_scale, down, down_scale)


def xor_pairs(size, step):
    return [(i, i ^ step) for i in range(size)]


def shards(tokens, expert_ids, gate_weights, w_gate_up, gate_up_scales, w_down, down_scales):
    node_count = lax.axis_size("node")
    local_count = lax.axis_size("local")
    chip_count = local_count // 2
    row_count, width = tokens.shape
    slice_count = local_count // EXP_GROUP
    over_node = lambda v, d: lax.ppermute(v, "node", xor_pairs(node_count, d))
    over_local = lambda v, d: lax.ppermute(v, "local", xor_pairs(local_count, d))
    add = lambda a, b: a.astype(jnp.float32) + b.astype(jnp.float32)

    which = (lax.axis_index("node") * EXP_GROUP + lax.axis_index("local") // slice_count).astype(jnp.int32)[None]
    up = pltpu.with_memory_space_constraint(w_gate_up[0], pltpu.VMEM)
    down = pltpu.with_memory_space_constraint(w_down[0], pltpu.VMEM)
    up_scale = jnp.repeat(gate_up_scales[0], BLOCK, axis=1)
    down_scale = jnp.repeat(down_scales[0], BLOCK, axis=1)

    packed = pack_rows(tokens, expert_ids, gate_weights)
    from_node = [packed] + [None] * (node_count - 1)
    for dz in range(node_count - 1, 0, -1):
        from_node[dz] = over_node(packed, dz)
    half_nodes = node_count // 2
    groups = [[node_count - 1 - i for i in range(half_nodes // 2)] + list(range(half_nodes // 2)), []]
    groups[1] = [dz for dz in range(node_count - 1, -1, -1) if dz not in groups[0]]

    returned = []
    for group in groups:
        same_core = []
        for dz in group:
            same_core.append(from_node[dz])
            for dx in range(1, chip_count):
                same_core.append(over_local(from_node[dz], 2 * dx))
        same_core = jnp.concatenate(same_core, axis=0)
        rows = jnp.concatenate([same_core, over_local(same_core, 1)], axis=0)
        outputs = expert_apply(which, rows, up, up_scale, down, down_scale)
        outputs = outputs.reshape(2, len(group), chip_count, row_count, width)
        for i, dz in enumerate(group):
            chip_sum = add(outputs[0, i], over_local(outputs[1, i], 1)).astype(jnp.bfloat16)
            partial = chip_sum[0].astype(jnp.float32)
            for dx in range(1, chip_count):
                partial = partial + over_local(chip_sum[dx], 2 * dx).astype(jnp.float32)
            partial = partial.astype(jnp.bfloat16)
            returned.append(over_node(partial, dz) if dz else partial)
    combined = functools.reduce(jnp.add, [v.astype(jnp.float32) for v in returned])
    return combined.astype(jnp.bfloat16)


def solution(mesh):
    rows = P(("parts", "node", "local"), None)
    held = P(("node", "local"), None, None)
    return jax.shard_map(
        shards,
        mesh=mesh,
        in_specs=(rows, rows, rows, held, held, held, held),
        out_specs=rows,
        check_vma=False,
    )
```

time: 85.6 us -> 88.7 us (1.036)
  blocking collectives: 28.5 us -> 0 us
  Pallas kernels: 0 us -> 24.3 us
  matrix products: 22.1 us -> 0 us
  local copies, waits for them, and re-layouts: 4.53 us -> 23.2 us
  starting transfers between devices: 7.36 us -> 24.2 us
  waiting for transfers between devices: 18.8 us -> 13.3 us
    all_to_all x1 -> x0, blocking collectives: 28.5 us -> none  [shards(): lax.all_to_all(outputs.reshape(full_shape), ('node', 'local'), split_axis...]
    pallas_call x0 -> x3, Pallas kernels: none -> 24.3 us  [the longest x2 22.6 us: expert_apply(): pl.pallas_call(expert_kernel, out_shape=jax.ShapeDtypeStruct((count, widt...]
    ppermute x0 -> x20, starting transfers between devices: none -> 24.2 us  [the longest x14 13.1 us: shards(): lax.ppermute(v, 'local', xor_pairs(local_count, d))]
    dot_general x7 -> x0, matrix products: 22.1 us -> none  [the longest x2 19.8 us: one_block(): jnp.einsum('mkc,kcn->mkn', row_block.reshape(row_block.shape[0], inner //...]
    all_to_all x1 -> x0, waiting for transfers between devices: 18.8 us -> none  [shards(): lax.all_to_all(send_rows, ('node', 'local'), split_axis=0, concat_axis=0,...]
    unnamed x3 -> x19, local copies, waits for them, and re-layouts: 0.15 us -> 18.3 us
    ppermute x0 -> x20, waiting for transfers between devices: none -> 13.3 us  [the longest x14 7.16 us: shards(): lax.ppermute(v, 'local', xor_pairs(local_count, d))]
    all_to_all x1 -> x0, starting transfers between devices: 7.36 us -> none  [shards(): lax.all_to_all(send_rows, ('node', 'local'), split_axis=0, concat_axis=0,...]
  transfers between devices with their start and end apart: 1 -> 20, of which waited for: 1 -> 8; matrix products, arithmetic and copies ran while one was open for 2% -> 10% of each run, Pallas kernels for 0% -> 26%
where the time goes in v1:
time: 88.7 us; the launch traced here: 88.3 us
  Pallas kernels  24.3 us (27%)
  starting transfers between devices  24.2 us (27%)
  local copies, waits for them, and re-layouts  23.2 us (26%)
  waiting for transfers between devices  13.3 us (15%)
  other arithmetic  3.04 us (3%)
    pallas_call x2, Pallas kernels, expert_apply(): pl.pallas_call(expert_kernel, out_shape=jax.ShapeDtypeStruct((count, widt...  22.6 us
    unnamed x19, local copies, waits for them, and re-layouts  18.3 us
    ppermute x14, starting transfers between devices, shards(): lax.ppermute(v, 'local', xor_pairs(local_count, d))  13.1 us
    ppermute x6, starting transfers between devices, shards(): over_node = lambda v, d: lax.ppermute(v, 'node', xor_pairs(node_count, d))  11.2 us
    ppermute x14, waiting for transfers between devices, shards(): lax.ppermute(v, 'local', xor_pairs(local_count, d))  7.16 us
    ppermute x6, waiting for transfers between devices, shards(): over_node = lambda v, d: lax.ppermute(v, 'node', xor_pairs(node_count, d))  6.11 us
    squeeze x2, local copies, waits for them, and re-layouts, shards(): outputs[1, i]  2.24 us
  transfers between devices with their start and end apart: 20, of which 8 were waited for; matrix products, arithmetic and copies ran while one was open for 10% of the time, Pallas kernels for 26%

profile of v1, /device:TPU:0, one launch (start us, length us, event | category | flops | bytes accessed | tf_op | source)
XLA Modules:
  0.0 88.3 jit_solution(12999470244547946081)
XLA Ops:
  0.0 1.7 %shard_map.73 = bf16[8,7296]{1,0:T(8,128)(2,1)} custom-call(bf16[8,7168]{1,0:T(8,128)(2,1)} %tokens_ref.1, s32[8,8]{1,0:T(8,128)} %ids_ref.1, bf16[8,8]{1,0:T(8,128)(2,1)} %gates_ref.1), custom_call_target="tpu_custom_call" | custom-call | tf_op jit(solution)/shard_map/pallas_call | solution.py:31
  1.7 4.0 %collective-permute-start.9 = (bf16[8,7296]{1,0:T(8,128)(2,1)}, bf16[8,7296]{1,0:T(8,128)(2,1)S(1)}, u32[]{:S(2)}, u32[]{:S(2)}) collective-permute-start(bf16[8,7296]{1,0:T(8,128)(2,1)} %shard_map.73), channel_id=1, source_target_pairs={{0,8},{4,12},{8,0},{12,4},{1,9},{5,13},{9,1},{13,5},{2,10},{6,14},... | collective-permute-start | bytes 350216 | tf_op jit(solution)/shard_map/ppermute | solution.py:116
  5.7 1.6 %collective-permute-start.11 = (bf16[8,7296]{1,0:T(8,128)(2,1)}, bf16[8,7296]{1,0:T(8,128)(2,1)S(1)}, u32[]{:S(2)}, u32[]{:S(2)}) collective-permute-start(bf16[8,7296]{1,0:T(8,128)(2,1)} %shard_map.73), channel_id=1, source_target_pairs={{0,4},{4,0},{8,12},{12,8},{1,5},{5,1},{9,13},{13,9},{2,6},{6,2},{1... | collective-permute-start | bytes 350216 | tf_op jit(solution)/shard_map/ppermute | solution.py:116
  7.3 1.7 %collective-permute-start.2 = (bf16[8,7296]{1,0:T(8,128)(2,1)}, bf16[8,7296]{1,0:T(8,128)(2,1)S(1)}, u32[]{:S(2)}, u32[]{:S(2)}) collective-permute-start(bf16[8,7296]{1,0:T(8,128)(2,1)} %shard_map.73), channel_id=1, source_target_pairs={{0,2},{1,3},{2,0},{3,1},{4,6},{5,7},{6,4},{7,5},{8,10},{9,11},{10,... | collective-permute-start | bytes 350216 | tf_op jit(solution)/shard_map/ppermute | solution.py:117
  13.3 3.6 %collective-permute-start.10 = (bf16[8,7296]{1,0:T(8,128)(2,1)S(1)}, bf16[8,7296]{1,0:T(8,128)(2,1)S(1)}, u32[]{:S(2)}, u32[]{:S(2)}) collective-permute-start(bf16[8,7296]{1,0:T(8,128)(2,1)S(1)} %collective-permute-done.9), channel_id=1, source_target_pairs={{0,2},{1,3},{2,0},{3,1},{4,6},{5,7},{6,4},{7,5},{8,10},{9,11},{10,... | collective-permute-start | bytes 350216 | tf_op jit(solution)/shard_map/ppermute | solution.py:117
  17.0 2.0 %collective-permute-start.1 = (bf16[8,7296]{1,0:T(8,128)(2,1)S(1)}, bf16[8,7296]{1,0:T(8,128)(2,1)S(1)}, u32[]{:S(2)}, u32[]{:S(2)}) collective-permute-start(bf16[8,7296]{1,0:T(8,128)(2,1)S(1)} %collective-permute-done), channel_id=1, source_target_pairs={{0,2},{1,3},{2,0},{3,1},{4,6},{5,7},{6,4},{7,5},{8,10},{9,11},{10,... | collective-permute-start | bytes 350216 | tf_op jit(solution)/shard_map/ppermute | solution.py:117
  19.6 2.0 %collective-permute-done.12 = bf16[8,7296]{1,0:T(8,128)(2,1)S(1)} collective-permute-done((bf16[8,7296]{1,0:T(8,128)(2,1)S(1)}, bf16[8,7296]{1,0:T(8,128)(2,1)S(1)}, u32[]{:S(2)}, u32[]{:S(2)}) %collective-permute-start.12) | collective-permute-done | bytes 116768 | tf_op jit(solution)/shard_map/ppermute | solution.py:117
  21.8 1.1 %collective-permute-done.1 = bf16[8,7296]{1,0:T(8,128)(2,1)S(1)} collective-permute-done((bf16[8,7296]{1,0:T(8,128)(2,1)S(1)}, bf16[8,7296]{1,0:T(8,128)(2,1)S(1)}, u32[]{:S(2)}, u32[]{:S(2)}) %collective-permute-start.1) | collective-permute-done | bytes 116768 | tf_op jit(solution)/shard_map/ppermute | solution.py:117
  23.9 0.9 %pad_maximum_fusion = bf16[32,7296]{1,0:T(8,128)(2,1)S(1)} fusion(bf16[8,7296]{1,0:T(8,128)(2,1)S(1)} %collective-permute-done.2, bf16[8,7296]{1,0:T(8,128)(2,1)} %shard_map.73, bf16[8,7296]{1,0:T(8,128)(2,1)S(1)} %collective-permute-done.1, bf16[8,7296]{1,0:T(8,128)(2,1)S(1)} %collective-permute-done), kind=kLoop, calls=%fused_computation | loop fusion | flops 1867776 | bytes 933888 | tf_op jit(solution)/shard_map/concatenate | solution.py:141
  25.0 0.9 %copy-done.3 = bf16[64,7296]{1,0:T(8,128)(2,1)} copy-done((bf16[64,7296]{1,0:T(8,128)(2,1)}, bf16[64,7296]{1,0:T(8,128)(2,1)S(1)}, u32[]{:S(2)}) %copy-start.3) | copy-done | bytes 933912
  26.0 9.3 %copy-done = bf16[1,7168,2048]{2,1,0:T(8,128)(2,1)S(1)} copy-done((bf16[1,7168,2048]{2,1,0:T(8,128)(2,1)S(1)}, bf16[1,7168,2048]{2,1,0:T(8,128)(2,1)}, u32[]{:S(2)}) %copy-start) | copy-done | bytes 29360152
  35.3 5.2 %copy-done.1 = bf16[1,1024,7168]{2,1,0:T(8,128)(2,1)S(1)} copy-done((bf16[1,1024,7168]{2,1,0:T(8,128)(2,1)S(1)}, bf16[1,1024,7168]{2,1,0:T(8,128)(2,1)}, u32[]{:S(2)}) %copy-start.1) | copy-done | bytes 14680088
  40.5 11.3 %shard_map.75 = bf16[64,7168]{1,0:T(8,128)(2,1)} custom-call(s32[1]{0:T(128)} %bitcast.which_ref, bf16[64,7296]{1,0:T(8,128)(2,1)} %copy-done.3, bf16[7168,2048]{1,0:T(8,128)(2,1)S(1)} %bitcast.69, f32[56,2048]{1,0:T(8,128)} %bitcast.73, bf16[1024,7168]{1,0:T(8,128)(2,1)S(1)} %bitcast.71, f32[8,7168]{1,0:T(8,128)} %broadcast_bitcast_fusion.down_scale_ref), custom_call_target="tpu_custom_call" | custom-call | flops 2818572288 | bytes 44040192 | tf_op jit(solution)/shard_map/pallas_call | solution.py:90
  51.8 1.2 %slice_bitcast_fusion.2 = (bf16[2,8,7168]{2,1,0:T(8,128)(2,1)S(1)}, bf16[2,8,7168]{2,1,0:T(8,128)(2,1)S(1)}) fusion(bf16[2,2,2,8,7168]{4,3,2,1,0:T(8,128)(2,1)} %bitcast.77), kind=kLoop, calls=%fused_computation.13 | loop fusion | bytes 917504 | tf_op jit(solution)/shard_map/squeeze | solution.py:146
  53.7 0.9 %copy-done.4 = bf16[64,7296]{1,0:T(8,128)(2,1)} copy-done((bf16[64,7296]{1,0:T(8,128)(2,1)}, bf16[64,7296]{1,0:T(8,128)(2,1)S(1)}, u32[]{:S(2)}) %copy-start.4) | copy-done | bytes 933912
  54.6 11.3 %shard_map.74 = bf16[64,7168]{1,0:T(8,128)(2,1)} custom-call(s32[1]{0:T(128)} %bitcast.which_ref, bf16[64,7296]{1,0:T(8,128)(2,1)} %copy-done.4, bf16[7168,2048]{1,0:T(8,128)(2,1)S(1)} %bitcast.70, f32[56,2048]{1,0:T(8,128)} %bitcast.74, bf16[1024,7168]{1,0:T(8,128)(2,1)S(1)} %bitcast.72, f32[8,7168]{1,0:T(8,128)} %broadcast_bitcast_fusion.down_scale_ref), custom_call_target="tpu_custom_call" | custom-call | flops 2818572288 | bytes 44040192 | tf_op jit(solution)/shard_map/pallas_call | solution.py:90
  66.0 1.1 %slice_bitcast_fusion.4 = (bf16[2,8,7168]{2,1,0:T(8,128)(2,1)S(1)}, bf16[2,8,7168]{2,1,0:T(8,128)(2,1)S(1)}) fusion(bf16[2,2,2,8,7168]{4,3,2,1,0:T(8,128)(2,1)} %bitcast.75), kind=kLoop, calls=%fused_computation.15 | loop fusion | bytes 917504 | tf_op jit(solution)/shard_map/squeeze | solution.py:146
  67.8 1.3 %collective-permute-start.18 = (bf16[8,7168]{1,0:T(8,128)(2,1)S(1)}, bf16[8,7168]{1,0:T(8,128)(2,1)S(1)}, u32[]{:S(2)}, u32[]{:S(2)}) collective-permute-start(bf16[8,7168]{1,0:T(8,128)(2,1)S(1)} %slice_bitcast_fusion.8), channel_id=1, source_target_pairs={{0,2},{1,3},{2,0},{3,1},{4,6},{5,7},{6,4},{7,5},{8,10},{9,11},{10,... | collective-permute-start | bytes 344072 | tf_op jit(solution)/shard_map/ppermute | solution.py:117
  69.9 1.2 %fusion.2 = (bf16[2,8,7168]{2,1,0:T(8,128)(2,1)S(1)}, bf16[2,8,7168]{2,1,0:T(8,128)(2,1)S(1)}) fusion(bf16[2,8,7168]{2,1,0:T(8,128)(2,1)S(1)} %collective-permute-done.7, bf16[2,2,2,8,7168]{4,3,2,1,0:T(8,128)(2,1)} %bitcast.76, bf16[2,8,7168]{2,1,0:T(8,128)(2,1)S(1)} %collective-permute-done.4), kind=kLoop, calls=%fused_computation.8 | loop fusion | flops 917504 | bytes 1376256 | tf_op jit(solution)/shard_map/convert_element_type | solution.py:146
  71.1 1.3 %collective-permute-start.5 = (bf16[8,7168]{1,0:T(8,128)(2,1)S(1)}, bf16[8,7168]{1,0:T(8,128)(2,1)S(1)}, u32[]{:S(2)}, u32[]{:S(2)}) collective-permute-start(bf16[8,7168]{1,0:T(8,128)(2,1)S(1)} %slice_bitcast_fusion.14), channel_id=1, source_target_pairs={{0,2},{1,3},{2,0},{3,1},{4,6},{5,7},{6,4},{7,5},{8,10},{9,11},{10,... | collective-permute-start | bytes 344072 | tf_op jit(solution)/shard_map/ppermute | solution.py:117
  74.1 2.1 %collective-permute-done.15 = bf16[8,7168]{1,0:T(8,128)(2,1)S(1)} collective-permute-done((bf16[8,7168]{1,0:T(8,128)(2,1)S(1)}, bf16[8,7168]{1,0:T(8,128)(2,1)S(1)}, u32[]{:S(2)}, u32[]{:S(2)}) %collective-permute-start.15) | collective-permute-done | bytes 114720 | tf_op jit(solution)/shard_map/ppermute | solution.py:117
  76.3 1.7 %collective-permute-start.16 = (bf16[8,7168]{1,0:T(8,128)(2,1)S(1)}, bf16[8,7168]{1,0:T(8,128)(2,1)S(1)}, u32[]{:S(2)}, u32[]{:S(2)}) collective-permute-start(bf16[8,7168]{1,0:T(8,128)(2,1)S(1)} %fusion.5), channel_id=1, source_target_pairs={{0,8},{4,12},{8,0},{12,4},{1,9},{5,13},{9,1},{13,5},{2,10},{6,14},... | collective-permute-start | bytes 344072 | tf_op jit(solution)/shard_map/ppermute | solution.py:116
  78.7 3.5 %collective-permute-start.6 = (bf16[8,7168]{1,0:T(8,128)(2,1)S(1)}, bf16[8,7168]{1,0:T(8,128)(2,1)S(1)}, u32[]{:S(2)}, u32[]{:S(2)}) collective-permute-start(bf16[8,7168]{1,0:T(8,128)(2,1)S(1)} %fusion.7), channel_id=1, source_target_pairs={{0,12},{4,8},{8,4},{12,0},{1,13},{5,9},{9,5},{13,1},{2,14},{6,10},... | collective-permute-start | bytes 344072 | tf_op jit(solution)/shard_map/ppermute | solution.py:116
  82.2 5.3 %collective-permute-done.16 = bf16[8,7168]{1,0:T(8,128)(2,1)S(1)} collective-permute-done((bf16[8,7168]{1,0:T(8,128)(2,1)S(1)}, bf16[8,7168]{1,0:T(8,128)(2,1)S(1)}, u32[]{:S(2)}, u32[]{:S(2)}) %collective-permute-start.16) | collective-permute-done | bytes 114720 | tf_op jit(solution)/shard_map/ppermute | solution.py:116
  (58 shorter events, 11.7 us)
Async XLA Ops:
  1.7 11.6 %collective-permute-start.9 = (bf16[8,7296]{1,0:T(8,128)(2,1)}, bf16[8,7296]{1,0:T(8,128)(2,1)S(1)}, u32[]{:S(2)}, u32[]{:S(2)}) collective-permute-start(bf16[8,7296]{1,0:T(8,128)(2,1)} %shard_map.73), channel_id=1, source_target_pairs={{0,8},{4,12},{8,0},{12,4},{1,9},{5,13},{9,1},{13,5},{2,10},{6,14},... | collective-permute-start | bytes 350216 | tf_op jit(solution)/shard_map/ppermute | solution.py:116
  5.7 11.2 %collective-permute-start.11 = (bf16[8,7296]{1,0:T(8,128)(2,1)}, bf16[8,7296]{1,0:T(8,128)(2,1)S(1)}, u32[]{:S(2)}, u32[]{:S(2)}) collective-permute-start(bf16[8,7296]{1,0:T(8,128)(2,1)} %shard_map.73), channel_id=1, source_target_pairs={{0,4},{4,0},{8,12},{12,8},{1,5},{5,1},{9,13},{13,9},{2,6},{6,2},{1... | collective-permute-start | bytes 350216 | tf_op jit(solution)/shard_map/ppermute | solution.py:116
  7.3 9.7 %collective-permute-start = (bf16[8,7296]{1,0:T(8,128)(2,1)}, bf16[8,7296]{1,0:T(8,128)(2,1)S(1)}, u32[]{:S(2)}, u32[]{:S(2)}) collective-permute-start(bf16[8,7296]{1,0:T(8,128)(2,1)} %shard_map.73), channel_id=1, source_target_pairs={{0,12},{4,8},{8,4},{12,0},{1,13},{5,9},{9,5},{13,1},{2,14},{6,10},... | collective-permute-start | bytes 350216 | tf_op jit(solution)/shard_map/ppermute | solution.py:116
  7.3 16.6 %collective-permute-start.2 = (bf16[8,7296]{1,0:T(8,128)(2,1)}, bf16[8,7296]{1,0:T(8,128)(2,1)S(1)}, u32[]{:S(2)}, u32[]{:S(2)}) collective-permute-start(bf16[8,7296]{1,0:T(8,128)(2,1)} %shard_map.73), channel_id=1, source_target_pairs={{0,2},{1,3},{2,0},{3,1},{4,6},{5,7},{6,4},{7,5},{8,10},{9,11},{10,... | collective-permute-start | bytes 350216 | tf_op jit(solution)/shard_map/ppermute | solution.py:117
  13.3 6.4 %collective-permute-start.10 = (bf16[8,7296]{1,0:T(8,128)(2,1)S(1)}, bf16[8,7296]{1,0:T(8,128)(2,1)S(1)}, u32[]{:S(2)}, u32[]{:S(2)}) collective-permute-start(bf16[8,7296]{1,0:T(8,128)(2,1)S(1)} %collective-permute-done.9), channel_id=1, source_target_pairs={{0,2},{1,3},{2,0},{3,1},{4,6},{5,7},{6,4},{7,5},{8,10},{9,11},{10,... | collective-permute-start | bytes 350216 | tf_op jit(solution)/shard_map/ppermute | solution.py:117
  16.9 4.8 %collective-permute-start.12 = (bf16[8,7296]{1,0:T(8,128)(2,1)S(1)}, bf16[8,7296]{1,0:T(8,128)(2,1)S(1)}, u32[]{:S(2)}, u32[]{:S(2)}) collective-permute-start(bf16[8,7296]{1,0:T(8,128)(2,1)S(1)} %collective-permute-done.11), channel_id=1, source_target_pairs={{0,2},{1,3},{2,0},{3,1},{4,6},{5,7},{6,4},{7,5},{8,10},{9,11},{10,... | collective-permute-start | bytes 350216 | tf_op jit(solution)/shard_map/ppermute | solution.py:117
  17.0 6.0 %collective-permute-start.1 = (bf16[8,7296]{1,0:T(8,128)(2,1)S(1)}, bf16[8,7296]{1,0:T(8,128)(2,1)S(1)}, u32[]{:S(2)}, u32[]{:S(2)}) collective-permute-start(bf16[8,7296]{1,0:T(8,128)(2,1)S(1)} %collective-permute-done), channel_id=1, source_target_pairs={{0,2},{1,3},{2,0},{3,1},{4,6},{5,7},{6,4},{7,5},{8,10},{9,11},{10,... | collective-permute-start | bytes 350216 | tf_op jit(solution)/shard_map/ppermute | solution.py:117
  21.7 3.2 %collective-permute-start.13 = (bf16[32,7296]{1,0:T(8,128)(2,1)S(1)}, bf16[32,7296]{1,0:T(8,128)(2,1)S(1)}, u32[]{:S(2)}, u32[]{:S(2)}) collective-permute-start(bf16[32,7296]{1,0:T(8,128)(2,1)S(1)} %pad_maximum_fusion.1), channel_id=1, source_target_pairs={{0,1},{1,0},{2,3},{3,2},{4,5},{5,4},{6,7},{7,6},{8,9},{9,8},{10,11... | collective-permute-start | bytes 1400840 | tf_op jit(solution)/shard_map/ppermute | solution.py:117
  24.8 28.8 %collective-permute-start.3 = (bf16[32,7296]{1,0:T(8,128)(2,1)S(1)}, bf16[32,7296]{1,0:T(8,128)(2,1)S(1)}, u32[]{:S(2)}, u32[]{:S(2)}) collective-permute-start(bf16[32,7296]{1,0:T(8,128)(2,1)S(1)} %pad_maximum_fusion), channel_id=1, source_target_pairs={{0,1},{1,0},{2,3},{3,2},{4,5},{5,4},{6,7},{7,6},{8,9},{9,8},{10,11... | collective-permute-start | bytes 1400840 | tf_op jit(solution)/shard_map/ppermute | solution.py:117
  25.0 1.0 %copy-start.3 = (bf16[64,7296]{1,0:T(8,128)(2,1)}, bf16[64,7296]{1,0:T(8,128)(2,1)S(1)}, u32[]{:S(2)}) copy-start(bf16[64,7296]{1,0:T(8,128)(2,1)S(1)} %constant_dynamic-update-slice_fusion.5.rows_ref) | copy-start | bytes 2801668
  26.0 9.4 %copy-start = (bf16[1,7168,2048]{2,1,0:T(8,128)(2,1)S(1)}, bf16[1,7168,2048]{2,1,0:T(8,128)(2,1)}, u32[]{:S(2)}) copy-start(bf16[1,7168,2048]{2,1,0:T(8,128)(2,1)} %param.10) | copy-start | bytes 88080384
  35.3 5.2 %copy-start.1 = (bf16[1,1024,7168]{2,1,0:T(8,128)(2,1)S(1)}, bf16[1,1024,7168]{2,1,0:T(8,128)(2,1)}, u32[]{:S(2)}) copy-start(bf16[1,1024,7168]{2,1,0:T(8,128)(2,1)} %param.12) | copy-start | bytes 44040196
  51.8 15.8 %copy-start.2 = (bf16[64,7168]{1,0:T(8,128)(2,1)S(1)}, bf16[64,7168]{1,0:T(8,128)(2,1)}, u32[]{:S(2)}) copy-start(bf16[64,7168]{1,0:T(8,128)(2,1)} %shard_map.75) | copy-start | bytes 2752516
  53.0 14.6 %collective-permute-start.14 = (bf16[2,8,7168]{2,1,0:T(8,128)(2,1)S(1)}, bf16[2,8,7168]{2,1,0:T(8,128)(2,1)S(1)}, u32[]{:S(2)}, u32[]{:S(2)}) collective-permute-start(bf16[2,8,7168]{2,1,0:T(8,128)(2,1)S(1)} %get-tuple-element.11), channel_id=1, source_target_pairs={{0,1},{1,0},{2,3},{3,2},{4,5},{5,4},{6,7},{7,6},{8,9},{9,8},{10,11... | collective-permute-start | bytes 688136 | tf_op jit(solution)/shard_map/ppermute | solution.py:117
  53.5 14.1 %collective-permute-start.17 = (bf16[2,8,7168]{2,1,0:T(8,128)(2,1)S(1)}, bf16[2,8,7168]{2,1,0:T(8,128)(2,1)S(1)}, u32[]{:S(2)}, u32[]{:S(2)}) collective-permute-start(bf16[2,8,7168]{2,1,0:T(8,128)(2,1)S(1)} %get-tuple-element.12), channel_id=1, source_target_pairs={{0,1},{1,0},{2,3},{3,2},{4,5},{5,4},{6,7},{7,6},{8,9},{9,8},{10,11... | collective-permute-start | bytes 688136 | tf_op jit(solution)/shard_map/ppermute | solution.py:117
  67.0 2.9 %collective-permute-start.7 = (bf16[2,8,7168]{2,1,0:T(8,128)(2,1)S(1)}, bf16[2,8,7168]{2,1,0:T(8,128)(2,1)S(1)}, u32[]{:S(2)}, u32[]{:S(2)}) collective-permute-start(bf16[2,8,7168]{2,1,0:T(8,128)(2,1)S(1)} %get-tuple-element.7), channel_id=1, source_target_pairs={{0,1},{1,0},{2,3},{3,2},{4,5},{5,4},{6,7},{7,6},{8,9},{9,8},{10,11... | collective-permute-start | bytes 688136 | tf_op jit(solution)/shard_map/ppermute | solution.py:117
  67.5 2.4 %collective-permute-start.4 = (bf16[2,8,7168]{2,1,0:T(8,128)(2,1)S(1)}, bf16[2,8,7168]{2,1,0:T(8,128)(2,1)S(1)}, u32[]{:S(2)}, u32[]{:S(2)}) collective-permute-start(bf16[2,8,7168]{2,1,0:T(8,128)(2,1)S(1)} %get-tuple-element.8), channel_id=1, source_target_pairs={{0,1},{1,0},{2,3},{3,2},{4,5},{5,4},{6,7},{7,6},{8,9},{9,8},{10,11... | collective-permute-start | bytes 688136 | tf_op jit(solution)/shard_map/ppermute | solution.py:117
  67.8 6.0 %collective-permute-start.18 = (bf16[8,7168]{1,0:T(8,128)(2,1)S(1)}, bf16[8,7168]{1,0:T(8,128)(2,1)S(1)}, u32[]{:S(2)}, u32[]{:S(2)}) collective-permute-start(bf16[8,7168]{1,0:T(8,128)(2,1)S(1)} %slice_bitcast_fusion.8), channel_id=1, source_target_pairs={{0,2},{1,3},{2,0},{3,1},{4,6},{5,7},{6,4},{7,5},{8,10},{9,11},{10,... | collective-permute-start | bytes 344072 | tf_op jit(solution)/shard_map/ppermute | solution.py:117
  69.1 7.1 %collective-permute-start.15 = (bf16[8,7168]{1,0:T(8,128)(2,1)S(1)}, bf16[8,7168]{1,0:T(8,128)(2,1)S(1)}, u32[]{:S(2)}, u32[]{:S(2)}) collective-permute-start(bf16[8,7168]{1,0:T(8,128)(2,1)S(1)} %slice_bitcast_fusion.10), channel_id=1, source_target_pairs={{0,2},{1,3},{2,0},{3,1},{4,6},{5,7},{6,4},{7,5},{8,10},{9,11},{10,... | collective-permute-start | bytes 344072 | tf_op jit(solution)/shard_map/ppermute | solution.py:117
  71.1 7.6 %collective-permute-start.5 = (bf16[8,7168]{1,0:T(8,128)(2,1)S(1)}, bf16[8,7168]{1,0:T(8,128)(2,1)S(1)}, u32[]{:S(2)}, u32[]{:S(2)}) collective-permute-start(bf16[8,7168]{1,0:T(8,128)(2,1)S(1)} %slice_bitcast_fusion.14), channel_id=1, source_target_pairs={{0,2},{1,3},{2,0},{3,1},{4,6},{5,7},{6,4},{7,5},{8,10},{9,11},{10,... | collective-permute-start | bytes 344072 | tf_op jit(solution)/shard_map/ppermute | solution.py:117
  72.4 9.8 %collective-permute-start.8 = (bf16[8,7168]{1,0:T(8,128)(2,1)S(1)}, bf16[8,7168]{1,0:T(8,128)(2,1)S(1)}, u32[]{:S(2)}, u32[]{:S(2)}) collective-permute-start(bf16[8,7168]{1,0:T(8,128)(2,1)S(1)} %slice_bitcast_fusion.12), channel_id=1, source_target_pairs={{0,2},{1,3},{2,0},{3,1},{4,6},{5,7},{6,4},{7,5},{8,10},{9,11},{10,... | collective-permute-start | bytes 344072 | tf_op jit(solution)/shard_map/ppermute | solution.py:117
  73.8 8.4 %collective-permute-start.19 = (bf16[8,7168]{1,0:T(8,128)(2,1)S(1)}, bf16[8,7168]{1,0:T(8,128)(2,1)S(1)}, u32[]{:S(2)}, u32[]{:S(2)}) collective-permute-start(bf16[8,7168]{1,0:T(8,128)(2,1)S(1)} %fusion.4), channel_id=1, source_target_pairs={{0,4},{4,0},{8,12},{12,8},{1,5},{5,1},{9,13},{13,9},{2,6},{6,2},{1... | collective-permute-start | bytes 344072 | tf_op jit(solution)/shard_map/ppermute | solution.py:116
  76.3 11.3 %collective-permute-start.16 = (bf16[8,7168]{1,0:T(8,128)(2,1)S(1)}, bf16[8,7168]{1,0:T(8,128)(2,1)S(1)}, u32[]{:S(2)}, u32[]{:S(2)}) collective-permute-start(bf16[8,7168]{1,0:T(8,128)(2,1)S(1)} %fusion.5), channel_id=1, source_target_pairs={{0,8},{4,12},{8,0},{12,4},{1,9},{5,13},{9,1},{13,5},{2,10},{6,14},... | collective-permute-start | bytes 344072 | tf_op jit(solution)/shard_map/ppermute | solution.py:116
  78.7 8.8 %collective-permute-start.6 = (bf16[8,7168]{1,0:T(8,128)(2,1)S(1)}, bf16[8,7168]{1,0:T(8,128)(2,1)S(1)}, u32[]{:S(2)}, u32[]{:S(2)}) collective-permute-start(bf16[8,7168]{1,0:T(8,128)(2,1)S(1)} %fusion.7), channel_id=1, source_target_pairs={{0,12},{4,8},{8,4},{12,0},{1,13},{5,9},{9,5},{13,1},{2,14},{6,10},... | collective-permute-start | bytes 344072 | tf_op jit(solution)/shard_map/ppermute | solution.py:116
  (1 other events, 1.0 us)

commit v2 on v1

v2 whole, which is shorter than its diff:
```python
import functools

import jax
import jax.numpy as jnp
from jax import lax
from jax.experimental import pallas as pl
from jax.experimental.pallas import tpu as pltpu
from jax.sharding import PartitionSpec as P

EXP_GROUP = 4
LANES = 128
LOADS = 4
BLOCK = 128
VMEM = pl.BlockSpec(memory_space=pltpu.VMEM)
HBM = pl.BlockSpec(memory_space=pltpu.HBM)


def pack_kernel(tokens_hbm, ids_hbm, gates_hbm, out_ref, ids_ref, gates_ref, sems):
    width = tokens_hbm.shape[1]
    rows = out_ref.shape[0]
    copies = [
        pltpu.make_async_copy(ids_hbm, ids_ref, sems.at[0]),
        pltpu.make_async_copy(gates_hbm, gates_ref, sems.at[1]),
        pltpu.make_async_copy(tokens_hbm, out_ref.at[:, pl.ds(0, width)], sems.at[2]),
    ]
    for copy in copies:
        copy.start()
    copies[0].wait()
    copies[1].wait()
    lane = lax.broadcasted_iota(jnp.int32, (rows, LANES), 1)
    ids = ids_ref[...]
    gates = gates_ref[...].astype(jnp.float32)
    route = jnp.zeros((rows, LANES), jnp.float32)
    for k in range(ids.shape[1]):
        route = route + jnp.where(ids[:, k : k + 1] == lane, gates[:, k : k + 1], 0.0)
    out_ref[:, width:] = route.astype(jnp.bfloat16)
    copies[2].wait()


def pack_rows(tokens, ids, gates):
    rows, width = tokens.shape
    return pl.pallas_call(
        pack_kernel,
        out_shape=pltpu.VMEM((rows, width + LANES), jnp.bfloat16),
        in_specs=[HBM, HBM, HBM],
        out_specs=VMEM,
        scratch_shapes=[
            pltpu.VMEM(ids.shape, ids.dtype),
            pltpu.VMEM(gates.shape, gates.dtype),
            pltpu.SemaphoreType.DMA((3,)),
        ],
        compiler_params=pltpu.CompilerParams(vmem_limit_bytes=2 << 20),
    )(in_hbm(tokens), in_hbm(ids), in_hbm(gates))


def tile_of(width, most=512):
    tile = min(width, most)
    while width % tile:
        tile -= BLOCK
    return tile


def spread(scales, contract, columns):
    blocks = columns // BLOCK
    col = lax.broadcasted_iota(jnp.int32, (blocks, columns), 1) // BLOCK
    row = lax.broadcasted_iota(jnp.int32, (blocks, columns), 0)
    wide = lax.dot_general(
        scales.astype(jnp.bfloat16),
        (col == row).astype(jnp.bfloat16),
        (((contract,), (0,)), ((), ())),
        preferred_element_type=jnp.float32,
    )
    return wide.astype(jnp.bfloat16)


def scales_kernel(up_scale_ref, down_scale_ref, up_wide_ref, down_wide_ref):
    up_wide_ref[...] = spread(up_scale_ref[...], 0, up_wide_ref.shape[1])
    down_wide_ref[...] = spread(down_scale_ref[...], 1, down_wide_ref.shape[1])


def spread_scales(up_scale, down_scale):
    return pl.pallas_call(
        scales_kernel,
        out_shape=[
            pltpu.VMEM((up_scale.shape[1], up_scale.shape[0] * BLOCK), jnp.bfloat16),
            pltpu.VMEM((down_scale.shape[0], down_scale.shape[1] * BLOCK), jnp.bfloat16),
        ],
        in_specs=[VMEM, VMEM],
        out_specs=[VMEM, VMEM],
        compiler_params=pltpu.CompilerParams(vmem_limit_bytes=4 << 20),
    )(up_scale, down_scale)


def load_kernel(start, weights_hbm, out_ref, sem):
    rows, columns = out_ref.shape
    copy = pltpu.make_async_copy(weights_hbm.at[pl.ds(start, rows), pl.ds(0, columns)], out_ref, sem)
    copy.start()
    copy.wait()


def load_rows(weights, start, rows, columns):
    return pl.pallas_call(
        functools.partial(load_kernel, start),
        out_shape=pltpu.VMEM((rows, columns), weights.dtype),
        in_specs=[HBM],
        out_specs=VMEM,
        scratch_shapes=[pltpu.SemaphoreType.DMA],
        compiler_params=pltpu.CompilerParams(vmem_limit_bytes=1 << 20),
        cost_estimate=pl.CostEstimate(flops=0, bytes_accessed=2 * rows * columns, transcendentals=0),
    )(in_hbm(weights))


def scaled(weights, scales):
    rows, columns = weights.shape
    blocks = weights.reshape(rows // BLOCK, BLOCK, columns) * scales[:, None, :]
    return blocks.reshape(rows, columns)


def expert_kernel(slice_count, pieces, rows_ref, *refs):
    gate_refs, refs = refs[:pieces], refs[pieces:]
    (up_scale_ref, down_scale_ref, pair_hbm, down_hbm, out_ref,
     up_ref, down_ref, hidden_ref, act_ref, up_sems, down_sems) = refs
    depth = pair_hbm.shape[0]
    half, width = down_hbm.shape
    tile, tile_out = tile_of(half), tile_of(width, 1024)
    steps, steps_out = half // tile, width // tile_out
    share = -(-steps_out // steps)
    band = depth // pieces

    def up_copy(i):
        return pltpu.make_async_copy(
            pair_hbm.at[:, pl.ds(half + i * tile, tile)], up_ref.at[:, pl.ds(i * tile, tile)], up_sems.at[i]
        )

    def down_copy(i):
        cols = pl.ds(i * tile_out, tile_out)
        return pltpu.make_async_copy(down_hbm.at[:, cols], down_ref.at[:, cols], down_sems.at[i])

    for i in range(steps):
        up_copy(i).start()
    for i in range(steps):
        cols = pl.ds(i * tile, tile)
        total = None
        for p in range(pieces):
            scales = up_scale_ref[p * band // BLOCK : (p + 1) * band // BLOCK, cols]
            part = jnp.dot(
                rows_ref[:, p * band : (p + 1) * band],
                scaled(gate_refs[p][:, cols], scales),
                preferred_element_type=jnp.float32,
            )
            total = part if total is None else total + part
        hidden_ref[:, cols] = total
    for i in range(steps):
        cols = pl.ds(i * tile, tile)
        up_copy(i).wait()
        for k in range(i * share, min(steps_out, i * share + share)):
            down_copy(k).start()
        weights = scaled(up_ref[:, cols], up_scale_ref[:, pl.ds(half + i * tile, tile)])
        other = jnp.dot(rows_ref[:, :depth], weights, preferred_element_type=jnp.float32)
        gate = hidden_ref[:, cols]
        act_ref[:, cols] = (gate / (1.0 + jnp.exp(-gate)) * other).astype(jnp.bfloat16)

    expert = lax.axis_index("node") * EXP_GROUP + lax.axis_index("local") // slice_count
    route = rows_ref[:, depth:].astype(jnp.float32)
    lane = lax.broadcasted_iota(jnp.int32, route.shape, 1)
    mine = jnp.sum(jnp.where(lane == expert, route, 0.0), axis=1, keepdims=True)
    for i in range(steps_out):
        cols = pl.ds(i * tile_out, tile_out)
        down_copy(i).wait()
        weights = scaled(down_ref[:, cols], down_scale_ref[:, cols])
        total = jnp.dot(act_ref[...], weights, preferred_element_type=jnp.float32)
        out_ref[:, cols] = jnp.where(mine > 0, total * mine, 0.0).astype(jnp.bfloat16)


def expert_apply(slice_count, rows, gates, up_scale, down_scale, pair, down):
    count = rows.shape[0]
    half, width = down.shape
    depth = pair.shape[0]
    pieces = len(gates)
    held = 2 * (depth * half + half * width + 3 * count * half)
    return pl.pallas_call(
        functools.partial(expert_kernel, slice_count, pieces),
        out_shape=pltpu.VMEM((count, width), jnp.bfloat16),
        in_specs=[VMEM] * (pieces + 3) + [HBM, HBM],
        out_specs=VMEM,
        scratch_shapes=[
            pltpu.VMEM((depth, half), jnp.bfloat16),
            pltpu.VMEM((half, width), jnp.bfloat16),
            pltpu.VMEM((count, half), jnp.float32),
            pltpu.VMEM((count, half), jnp.bfloat16),
            pltpu.SemaphoreType.DMA((half // tile_of(half),)),
            pltpu.SemaphoreType.DMA((width // tile_of(width, 1024),)),
        ],
        compiler_params=pltpu.CompilerParams(vmem_limit_bytes=held + (5 << 20) + 12 * 1024 * count),
        cost_estimate=pl.CostEstimate(
            flops=2 * count * (pair.size + down.size), bytes_accessed=pair.size + down.size, transcendentals=count * half
        ),
    )(
        in_vmem(rows), *map(in_vmem, gates), in_vmem(up_scale), in_vmem(down_scale), in_hbm(pair), in_hbm(down)
    )


def in_vmem(value):
    return pltpu.with_memory_space_constraint(value, pltpu.VMEM)


def in_hbm(value):
    return pltpu.with_memory_space_constraint(value, pltpu.HBM)


def xor_pairs(size, step):
    return [(i, i ^ step) for i in range(size)]


def shards(tokens, expert_ids, gate_weights, w_gate_up, gate_up_scales, w_down, down_scales):
    node_count = lax.axis_size("node")
    local_count = lax.axis_size("local")
    chip_count = local_count // 2
    row_count, width = tokens.shape
    slice_count = local_count // EXP_GROUP
    over_node = lambda v, d: lax.ppermute(v, "node", xor_pairs(node_count, d))
    over_local = lambda v, d: lax.ppermute(v, "local", xor_pairs(local_count, d))
    add = lambda a, b: a.astype(jnp.float32) + b.astype(jnp.float32)

    pair, down = w_gate_up[0], w_down[0]
    up_scale, down_scale = spread_scales(gate_up_scales[0].T, down_scales[0])
    band = pair.shape[0] // LOADS
    load = lambda source, i: load_rows(source, i * band, band, down.shape[0])
    gates = [load(pair, 0)] + [None] * (LOADS - 1)

    packed = pack_rows(tokens, expert_ids, gate_weights)
    from_node = [packed] + [None] * (node_count - 1)
    for dz in range(node_count - 1, 0, -1):
        from_node[dz] = over_node(packed, dz)
    group = [node_count - 1] + list(range(1, node_count - 1)) + [0]
    same_core = []
    for i, dz in enumerate(group):
        piece = from_node[dz]
        if i == 0:
            piece, gates[0] = lax.optimization_barrier((piece, gates[0]))
        others = [over_local(piece, 2 * dx) for dx in range(1, chip_count)]
        if i < LOADS - 2:
            others, later = lax.optimization_barrier((others, pair))
            gates[i + 1] = load(later, i + 1)
        same_core += [piece, *others]
    gates[-1] = load(pair, LOADS - 1)
    same_core, gates[1:-1] = lax.optimization_barrier((same_core, gates[1:-1]))
    same_core = jnp.concatenate(same_core, axis=0)
    rows = jnp.concatenate([same_core, over_local(same_core, 1)], axis=0)
    outputs = expert_apply(slice_count, rows, gates, up_scale, down_scale, pair, down)
    outputs = outputs.reshape(2, node_count, chip_count, row_count, width)
    returned = []
    for i, dz in enumerate(group):
        chip_sum = add(outputs[0, i], over_local(outputs[1, i], 1)).astype(jnp.bfloat16)
        partial = chip_sum[0].astype(jnp.float32)
        for dx in range(1, chip_count):
            partial = partial + over_local(chip_sum[dx], 2 * dx).astype(jnp.float32)
        partial = partial.astype(jnp.bfloat16)
        returned.append(over_node(partial, dz) if dz else partial)
    combined = functools.reduce(jnp.add, [v.astype(jnp.float32) for v in returned])
    return combined.astype(jnp.bfloat16)


def solution(mesh):
    rows = P(("parts", "node", "local"), None)
    held = P(("node", "local"), None, None)
    return jax.shard_map(
        shards,
        mesh=mesh,
        in_specs=(rows, rows, rows, held, held, held, held),
        out_specs=rows,
        check_vma=False,
    )
```

time: 88.7 us -> 59.5 us (0.67)
  local copies, waits for them, and re-layouts: 23.2 us -> 0.4 us
  Pallas kernels: 24.3 us -> 20.9 us
  starting transfers between devices: 24.2 us -> 21.1 us
  waiting for transfers between devices: 13.3 us -> 15.7 us
  other arithmetic: 3.04 us -> 1.03 us
    unnamed x19 -> x11, local copies, waits for them, and re-layouts: 18.3 us -> 0.17 us
    pallas_call x3 -> x7, Pallas kernels: 24.3 us -> 20.9 us  [the longest x1 11.4 us: expert_apply(): pl.pallas_call(functools.partial(expert_kernel, slice_count, pieces), out...]
    ppermute x6, waiting for transfers between devices: 6.11 us -> 9.38 us  [shards(): over_node = lambda v, d: lax.ppermute(v, 'node', xor_pairs(node_count, d))]
    ppermute x14 -> x13, starting transfers between devices: 13.1 us -> 10.7 us  [shards(): lax.ppermute(v, 'local', xor_pairs(local_count, d))]
    squeeze x2 -> x1, local copies, waits for them, and re-layouts: 2.24 us -> 0.06 us  [shards(): outputs[1, i]]
    squeeze x2 -> x0, local copies, waits for them, and re-layouts: 1.54 us -> none  [the longest x1 0.78 us: shards(): up_scale = jnp.repeat(gate_up_scales[0], BLOCK, axis=1)]
    convert_element_type x2 -> x1, other arithmetic: 1.27 us -> 0.21 us  [shards(): add(outputs[0, i], over_local(outputs[1, i], 1)).astype(jnp.bfloat16)]
    concatenate x2 -> x0, other arithmetic: 0.97 us -> none  [shards(): same_core = jnp.concatenate(same_core, axis=0)]
  transfers between devices with their start and end apart: 20 -> 19, of which waited for: 8 -> 16; matrix products, arithmetic and copies ran while one was open for 10% -> 0% of each run, Pallas kernels for 26% -> 14%
where the time goes in v2:
time: 59.5 us; the launch traced here: 59.3 us
  starting transfers between devices  21.1 us (35%)
  Pallas kernels  20.9 us (35%)
  waiting for transfers between devices  15.7 us (26%)
  other arithmetic  1.03 us (2%)
    pallas_call x1, Pallas kernels, expert_apply(): pl.pallas_call(functools.partial(expert_kernel, slice_count, pieces), out...  11.4 us
    ppermute x13, starting transfers between devices, shards(): lax.ppermute(v, 'local', xor_pairs(local_count, d))  10.7 us
    ppermute x6, starting transfers between devices, shards(): over_node = lambda v, d: lax.ppermute(v, 'node', xor_pairs(node_count, d))  10.4 us
    ppermute x6, waiting for transfers between devices, shards(): over_node = lambda v, d: lax.ppermute(v, 'node', xor_pairs(node_count, d))  9.38 us
    pallas_call x4, Pallas kernels, load_rows(): pl.pallas_call(functools.partial(load_kernel, start), out_shape=pltpu.VME...  8.19 us
    ppermute x13, waiting for transfers between devices, shards(): lax.ppermute(v, 'local', xor_pairs(local_count, d))  6.29 us
  transfers between devices with their start and end apart: 19, of which 16 were waited for; matrix products, arithmetic and copies ran while one was open for 0% of the time, Pallas kernels for 14%

profile of v2, /device:TPU:0, one launch (start us, length us, event | category | flops | bytes accessed | tf_op | source)
XLA Modules:
  0.0 59.3 jit_solution(432062918703488176)
XLA Ops:
  0.0 1.0 %shard_map.73 = bf16[8,7296]{1,0:T(8,128)(2,1)S(1)} custom-call(bf16[8,7168]{1,0:T(8,128)(2,1)} %tokens_hbm.1, s32[8,8]{1,0:T(8,128)} %ids_hbm.1, bf16[8,8]{1,0:T(8,128)(2,1)} %gates_hbm.1), custom_call_target="tpu_custom_call" | custom-call | tf_op jit(solution)/shard_map/pallas_call | solution.py:42
  1.0 5.1 %collective-permute-start = (bf16[8,7296]{1,0:T(8,128)(2,1)S(1)}, bf16[8,7296]{1,0:T(8,128)(2,1)S(1)}, u32[]{:S(2)}, u32[]{:S(2)}) collective-permute-start(bf16[8,7296]{1,0:T(8,128)(2,1)S(1)} %shard_map.73), channel_id=1, source_target_pairs={{0,12},{4,8},{8,4},{12,0},{1,13},{5,9},{9,5},{13,1},{2,14},{6,10},... | collective-permute-start | bytes 350216 | tf_op jit(solution)/shard_map/ppermute | solution.py:221
  6.1 0.6 %collective-permute-start.4 = (bf16[8,7296]{1,0:T(8,128)(2,1)S(1)}, bf16[8,7296]{1,0:T(8,128)(2,1)S(1)}, u32[]{:S(2)}, u32[]{:S(2)}) collective-permute-start(bf16[8,7296]{1,0:T(8,128)(2,1)S(1)} %shard_map.73), channel_id=1, source_target_pairs={{0,8},{4,12},{8,0},{12,4},{1,9},{5,13},{9,1},{13,5},{2,10},{6,14},... | collective-permute-start | bytes 350216 | tf_op jit(solution)/shard_map/ppermute | solution.py:221
  6.7 2.0 %shard_map.74.refs_0_ = bf16[1792,1024]{1,0:T(8,128)(2,1)S(1)} custom-call(bf16[7168,2048]{1,0:T(8,128)(2,1)} %bitcast.67), custom_call_target="tpu_custom_call" | custom-call | bytes 3670016 | tf_op jit(solution)/shard_map/pallas_call | solution.py:102
  8.8 1.4 %collective-permute-done = bf16[8,7296]{1,0:T(8,128)(2,1)S(1)} collective-permute-done((bf16[8,7296]{1,0:T(8,128)(2,1)S(1)}, bf16[8,7296]{1,0:T(8,128)(2,1)S(1)}, u32[]{:S(2)}, u32[]{:S(2)}) %collective-permute-start) | collective-permute-done | bytes 116768 | tf_op jit(solution)/shard_map/ppermute | solution.py:221
  10.1 1.7 %collective-permute-start.1 = (bf16[8,7296]{1,0:T(8,128)(2,1)S(1)}, bf16[8,7296]{1,0:T(8,128)(2,1)S(1)}, u32[]{:S(2)}, u32[]{:S(2)}) collective-permute-start(bf16[8,7296]{1,0:T(8,128)(2,1)S(1)} %collective-permute-done), channel_id=1, source_target_pairs={{0,2},{1,3},{2,0},{3,1},{4,6},{5,7},{6,4},{7,5},{8,10},{9,11},{10,... | collective-permute-start | bytes 350216 | tf_op jit(solution)/shard_map/ppermute | solution.py:222
  11.8 1.0 %collective-permute-done.2 = bf16[8,7296]{1,0:T(8,128)(2,1)S(1)} collective-permute-done((bf16[8,7296]{1,0:T(8,128)(2,1)S(1)}, bf16[8,7296]{1,0:T(8,128)(2,1)S(1)}, u32[]{:S(2)}, u32[]{:S(2)}) %collective-permute-start.2) | collective-permute-done | bytes 116768 | tf_op jit(solution)/shard_map/ppermute | solution.py:221
  12.9 1.4 %collective-permute-start.3 = (bf16[8,7296]{1,0:T(8,128)(2,1)S(1)}, bf16[8,7296]{1,0:T(8,128)(2,1)S(1)}, u32[]{:S(2)}, u32[]{:S(2)}) collective-permute-start(bf16[8,7296]{1,0:T(8,128)(2,1)S(1)} %collective-permute-done.2), channel_id=1, source_target_pairs={{0,2},{1,3},{2,0},{3,1},{4,6},{5,7},{6,4},{7,5},{8,10},{9,11},{10,... | collective-permute-start | bytes 350216 | tf_op jit(solution)/shard_map/ppermute | solution.py:222
  14.9 1.0 %collective-permute-done.4 = bf16[8,7296]{1,0:T(8,128)(2,1)S(1)} collective-permute-done((bf16[8,7296]{1,0:T(8,128)(2,1)S(1)}, bf16[8,7296]{1,0:T(8,128)(2,1)S(1)}, u32[]{:S(2)}, u32[]{:S(2)}) %collective-permute-start.4) | collective-permute-done | bytes 116768 | tf_op jit(solution)/shard_map/ppermute | solution.py:221
  15.9 1.5 %collective-permute-start.5 = (bf16[8,7296]{1,0:T(8,128)(2,1)S(1)}, bf16[8,7296]{1,0:T(8,128)(2,1)S(1)}, u32[]{:S(2)}, u32[]{:S(2)}) collective-permute-start(bf16[8,7296]{1,0:T(8,128)(2,1)S(1)} %collective-permute-done.4), channel_id=1, source_target_pairs={{0,2},{1,3},{2,0},{3,1},{4,6},{5,7},{6,4},{7,5},{8,10},{9,11},{10,... | collective-permute-start | bytes 350216 | tf_op jit(solution)/shard_map/ppermute | solution.py:222
  17.4 2.0 %shard_map.75.refs_1_ = bf16[1792,1024]{1,0:T(8,128)(2,1)S(1)} custom-call(bf16[7168,2048]{1,0:T(8,128)(2,1)} %bitcast.68), custom_call_target="tpu_custom_call" | custom-call | bytes 3670016 | tf_op jit(solution)/shard_map/pallas_call | solution.py:102
  19.5 2.1 %shard_map.76.refs_2_ = bf16[1792,1024]{1,0:T(8,128)(2,1)S(1)} custom-call(bf16[7168,2048]{1,0:T(8,128)(2,1)} %bitcast.69), custom_call_target="tpu_custom_call" | custom-call | bytes 3670016 | tf_op jit(solution)/shard_map/pallas_call | solution.py:102
  21.6 0.9 %collective-permute-done.5 = bf16[8,7296]{1,0:T(8,128)(2,1)S(1)} collective-permute-done((bf16[8,7296]{1,0:T(8,128)(2,1)S(1)}, bf16[8,7296]{1,0:T(8,128)(2,1)S(1)}, u32[]{:S(2)}, u32[]{:S(2)}) %collective-permute-start.5) | collective-permute-done | bytes 116768 | tf_op jit(solution)/shard_map/ppermute | solution.py:222
  22.8 2.1 %shard_map.77.refs_3_ = bf16[1792,1024]{1,0:T(8,128)(2,1)S(1)} custom-call(bf16[7168,2048]{1,0:T(8,128)(2,1)} %bitcast.70), custom_call_target="tpu_custom_call" | custom-call | bytes 3670016 | tf_op jit(solution)/shard_map/pallas_call | solution.py:102
  25.4 11.4 %shard_map.79 = bf16[128,7168]{1,0:T(8,128)(2,1)S(1)} custom-call(bf16[128,7296]{1,0:T(8,128)(2,1)S(1)} %constant_dynamic-update-slice_fusion.8.rows_ref, bf16[1792,1024]{1,0:T(8,128)(2,1)S(1)} %shard_map.74.refs_0_, bf16[1792,1024]{1,0:T(8,128)(2,1)S(1)} %shard_map.75.refs_1_, bf16[1792,1024]{1,0:T(8,128)(2,1)S(1)} %shard_map.76.refs_2_, ...), custom_call_target="tpu_custom_call" | custom-call | flops 5637144576 | bytes 22020096 | tf_op jit(solution)/shard_map/pallas_call | solution.py:181
  39.7 1.8 %collective-permute-start.9 = (bf16[8,7168]{1,0:T(8,128)(2,1)S(1)}, bf16[8,7168]{1,0:T(8,128)(2,1)S(1)}, u32[]{:S(2)}, u32[]{:S(2)}) collective-permute-start(bf16[8,7168]{1,0:T(8,128)(2,1)S(1)} %slice_bitcast_fusion.14), channel_id=1, source_target_pairs={{0,2},{1,3},{2,0},{3,1},{4,6},{5,7},{6,4},{7,5},{8,10},{9,11},{10,... | collective-permute-start | bytes 344072 | tf_op jit(solution)/shard_map/ppermute | solution.py:222
  41.9 1.8 %collective-permute-start.15 = (bf16[8,7168]{1,0:T(8,128)(2,1)S(1)}, bf16[8,7168]{1,0:T(8,128)(2,1)S(1)}, u32[]{:S(2)}, u32[]{:S(2)}) collective-permute-start(bf16[8,7168]{1,0:T(8,128)(2,1)S(1)} %slice_bitcast_fusion.10), channel_id=1, source_target_pairs={{0,2},{1,3},{2,0},{3,1},{4,6},{5,7},{6,4},{7,5},{8,10},{9,11},{10,... | collective-permute-start | bytes 344072 | tf_op jit(solution)/shard_map/ppermute | solution.py:222
  44.1 1.7 %collective-permute-done.9 = bf16[8,7168]{1,0:T(8,128)(2,1)S(1)} collective-permute-done((bf16[8,7168]{1,0:T(8,128)(2,1)S(1)}, bf16[8,7168]{1,0:T(8,128)(2,1)S(1)}, u32[]{:S(2)}, u32[]{:S(2)}) %collective-permute-start.9) | collective-permute-done | bytes 114720 | tf_op jit(solution)/shard_map/ppermute | solution.py:222
  45.8 2.1 %collective-permute-start.10 = (bf16[8,7168]{1,0:T(8,128)(2,1)S(1)}, bf16[8,7168]{1,0:T(8,128)(2,1)S(1)}, u32[]{:S(2)}, u32[]{:S(2)}) collective-permute-start(bf16[8,7168]{1,0:T(8,128)(2,1)S(1)} %fusion.7), channel_id=1, source_target_pairs={{0,12},{4,8},{8,4},{12,0},{1,13},{5,9},{9,5},{13,1},{2,14},{6,10},... | collective-permute-start | bytes 344072 | tf_op jit(solution)/shard_map/ppermute | solution.py:221
  48.3 1.9 %collective-permute-start.13 = (bf16[8,7168]{1,0:T(8,128)(2,1)S(1)}, bf16[8,7168]{1,0:T(8,128)(2,1)S(1)}, u32[]{:S(2)}, u32[]{:S(2)}) collective-permute-start(bf16[8,7168]{1,0:T(8,128)(2,1)S(1)} %fusion.6), channel_id=1, source_target_pairs={{0,4},{4,0},{8,12},{12,8},{1,5},{5,1},{9,13},{13,9},{2,6},{6,2},{1... | collective-permute-start | bytes 344072 | tf_op jit(solution)/shard_map/ppermute | solution.py:221
  51.3 1.2 %collective-permute-done.18 = bf16[8,7168]{1,0:T(8,128)(2,1)S(1)} collective-permute-done((bf16[8,7168]{1,0:T(8,128)(2,1)S(1)}, bf16[8,7168]{1,0:T(8,128)(2,1)S(1)}, u32[]{:S(2)}, u32[]{:S(2)}) %collective-permute-start.18) | collective-permute-done | bytes 114720 | tf_op jit(solution)/shard_map/ppermute | solution.py:222
  53.1 2.1 %collective-permute-done.13 = bf16[8,7168]{1,0:T(8,128)(2,1)S(1)} collective-permute-done((bf16[8,7168]{1,0:T(8,128)(2,1)S(1)}, bf16[8,7168]{1,0:T(8,128)(2,1)S(1)}, u32[]{:S(2)}, u32[]{:S(2)}) %collective-permute-start.13) | collective-permute-done | bytes 114720 | tf_op jit(solution)/shard_map/ppermute | solution.py:221
  55.2 3.3 %collective-permute-done.16 = bf16[8,7168]{1,0:T(8,128)(2,1)S(1)} collective-permute-done((bf16[8,7168]{1,0:T(8,128)(2,1)S(1)}, bf16[8,7168]{1,0:T(8,128)(2,1)S(1)}, u32[]{:S(2)}, u32[]{:S(2)}) %collective-permute-start.16) | collective-permute-done | bytes 114720 | tf_op jit(solution)/shard_map/ppermute | solution.py:221
  58.5 0.7 %add_convert_fusion = bf16[8,7168]{1,0:T(8,128)(2,1)} fusion(bf16[8,7168]{1,0:T(8,128)(2,1)S(1)} %collective-permute-done.16, bf16[8,7168]{1,0:T(8,128)(2,1)S(1)} %collective-permute-done.13, bf16[8,7168]{1,0:T(8,128)(2,1)S(1)} %collective-permute-done.10, bf16[8,7168]{1,0:T(8,128)(2,1)S(1)} %collective-permute-done.18, ...), kind=kLoop, calls=%fused_computation.24 | loop fusion | flops 688128 | bytes 688128 | tf_op jit(solution)/shard_map/convert_element_type | solution.py:261
  (44 shorter events, 7.2 us)
Async XLA Ops:
  1.0 9.2 %collective-permute-start = (bf16[8,7296]{1,0:T(8,128)(2,1)S(1)}, bf16[8,7296]{1,0:T(8,128)(2,1)S(1)}, u32[]{:S(2)}, u32[]{:S(2)}) collective-permute-start(bf16[8,7296]{1,0:T(8,128)(2,1)S(1)} %shard_map.73), channel_id=1, source_target_pairs={{0,12},{4,8},{8,4},{12,0},{1,13},{5,9},{9,5},{13,1},{2,14},{6,10},... | collective-permute-start | bytes 350216 | tf_op jit(solution)/shard_map/ppermute | solution.py:221
  6.1 6.8 %collective-permute-start.2 = (bf16[8,7296]{1,0:T(8,128)(2,1)S(1)}, bf16[8,7296]{1,0:T(8,128)(2,1)S(1)}, u32[]{:S(2)}, u32[]{:S(2)}) collective-permute-start(bf16[8,7296]{1,0:T(8,128)(2,1)S(1)} %shard_map.73), channel_id=1, source_target_pairs={{0,4},{4,0},{8,12},{12,8},{1,5},{5,1},{9,13},{13,9},{2,6},{6,2},{1... | collective-permute-start | bytes 350216 | tf_op jit(solution)/shard_map/ppermute | solution.py:221
  6.1 9.8 %collective-permute-start.4 = (bf16[8,7296]{1,0:T(8,128)(2,1)S(1)}, bf16[8,7296]{1,0:T(8,128)(2,1)S(1)}, u32[]{:S(2)}, u32[]{:S(2)}) collective-permute-start(bf16[8,7296]{1,0:T(8,128)(2,1)S(1)} %shard_map.73), channel_id=1, source_target_pairs={{0,8},{4,12},{8,0},{12,4},{1,9},{5,13},{9,1},{13,5},{2,10},{6,14},... | collective-permute-start | bytes 350216 | tf_op jit(solution)/shard_map/ppermute | solution.py:221
  10.1 7.3 %collective-permute-start.1 = (bf16[8,7296]{1,0:T(8,128)(2,1)S(1)}, bf16[8,7296]{1,0:T(8,128)(2,1)S(1)}, u32[]{:S(2)}, u32[]{:S(2)}) collective-permute-start(bf16[8,7296]{1,0:T(8,128)(2,1)S(1)} %collective-permute-done), channel_id=1, source_target_pairs={{0,2},{1,3},{2,0},{3,1},{4,6},{5,7},{6,4},{7,5},{8,10},{9,11},{10,... | collective-permute-start | bytes 350216 | tf_op jit(solution)/shard_map/ppermute | solution.py:222
  12.9 6.6 %collective-permute-start.3 = (bf16[8,7296]{1,0:T(8,128)(2,1)S(1)}, bf16[8,7296]{1,0:T(8,128)(2,1)S(1)}, u32[]{:S(2)}, u32[]{:S(2)}) collective-permute-start(bf16[8,7296]{1,0:T(8,128)(2,1)S(1)} %collective-permute-done.2), channel_id=1, source_target_pairs={{0,2},{1,3},{2,0},{3,1},{4,6},{5,7},{6,4},{7,5},{8,10},{9,11},{10,... | collective-permute-start | bytes 350216 | tf_op jit(solution)/shard_map/ppermute | solution.py:222
  14.3 7.3 %collective-permute-start.6 = (bf16[8,7296]{1,0:T(8,128)(2,1)S(1)}, bf16[8,7296]{1,0:T(8,128)(2,1)S(1)}, u32[]{:S(2)}, u32[]{:S(2)}) collective-permute-start(bf16[8,7296]{1,0:T(8,128)(2,1)S(1)} %shard_map.73), channel_id=1, source_target_pairs={{0,2},{1,3},{2,0},{3,1},{4,6},{5,7},{6,4},{7,5},{8,10},{9,11},{10,... | collective-permute-start | bytes 350216 | tf_op jit(solution)/shard_map/ppermute | solution.py:222
  15.9 6.5 %collective-permute-start.5 = (bf16[8,7296]{1,0:T(8,128)(2,1)S(1)}, bf16[8,7296]{1,0:T(8,128)(2,1)S(1)}, u32[]{:S(2)}, u32[]{:S(2)}) collective-permute-start(bf16[8,7296]{1,0:T(8,128)(2,1)S(1)} %collective-permute-done.4), channel_id=1, source_target_pairs={{0,2},{1,3},{2,0},{3,1},{4,6},{5,7},{6,4},{7,5},{8,10},{9,11},{10,... | collective-permute-start | bytes 350216 | tf_op jit(solution)/shard_map/ppermute | solution.py:222
  22.7 2.2 %copy-start = (f32[1,56,16]{1,2,0:T(8,128)S(1)}, f32[1,56,16]{1,2,0:T(8,128)}, u32[]{:S(2)}) copy-start(f32[1,56,16]{1,2,0:T(8,128)} %param.11) | copy-start | bytes 10756
  22.7 2.2 %copy-start.1 = (f32[1,8,56]{2,1,0:T(8,128)S(1)}, f32[1,8,56]{2,1,0:T(8,128)}, u32[]{:S(2)}) copy-start(f32[1,8,56]{2,1,0:T(8,128)} %param.13) | copy-start | bytes 5380
  22.7 2.6 %collective-permute-start.7 = (bf16[64,7296]{1,0:T(8,128)(2,1)S(1)}, bf16[64,7296]{1,0:T(8,128)(2,1)S(1)}, u32[]{:S(2)}, u32[]{:S(2)}) collective-permute-start(bf16[64,7296]{1,0:T(8,128)(2,1)S(1)} %get-tuple-element.49), channel_id=1, source_target_pairs={{0,1},{1,0},{2,3},{3,2},{4,5},{5,4},{6,7},{7,6},{8,9},{9,8},{10,11... | collective-permute-start | bytes 2801672 | tf_op jit(solution)/shard_map/ppermute | solution.py:222
  36.9 1.6 %collective-permute-start.11 = (bf16[2,8,7168]{2,1,0:T(8,128)(2,1)S(1)}, bf16[2,8,7168]{2,1,0:T(8,128)(2,1)S(1)}, u32[]{:S(2)}, u32[]{:S(2)}) collective-permute-start(bf16[2,8,7168]{2,1,0:T(8,128)(2,1)S(1)} %get-tuple-element.47), channel_id=1, source_target_pairs={{0,1},{1,0},{2,3},{3,2},{4,5},{5,4},{6,7},{7,6},{8,9},{9,8},{10,11... | collective-permute-start | bytes 688136 | tf_op jit(solution)/shard_map/ppermute | solution.py:222
  37.4 1.5 %collective-permute-start.14 = (bf16[2,8,7168]{2,1,0:T(8,128)(2,1)S(1)}, bf16[2,8,7168]{2,1,0:T(8,128)(2,1)S(1)}, u32[]{:S(2)}, u32[]{:S(2)}) collective-permute-start(bf16[2,8,7168]{2,1,0:T(8,128)(2,1)S(1)} %get-tuple-element.46), channel_id=1, source_target_pairs={{0,1},{1,0},{2,3},{3,2},{4,5},{5,4},{6,7},{7,6},{8,9},{9,8},{10,11... | collective-permute-start | bytes 688136 | tf_op jit(solution)/shard_map/ppermute | solution.py:222
  37.5 1.7 %collective-permute-start.17 = (bf16[2,8,7168]{2,1,0:T(8,128)(2,1)S(1)}, bf16[2,8,7168]{2,1,0:T(8,128)(2,1)S(1)}, u32[]{:S(2)}, u32[]{:S(2)}) collective-permute-start(bf16[2,8,7168]{2,1,0:T(8,128)(2,1)S(1)} %get-tuple-element.45), channel_id=1, source_target_pairs={{0,1},{1,0},{2,3},{3,2},{4,5},{5,4},{6,7},{7,6},{8,9},{9,8},{10,11... | collective-permute-start | bytes 688136 | tf_op jit(solution)/shard_map/ppermute | solution.py:222
  37.9 1.6 %collective-permute-start.8 = (bf16[2,8,7168]{2,1,0:T(8,128)(2,1)S(1)}, bf16[2,8,7168]{2,1,0:T(8,128)(2,1)S(1)}, u32[]{:S(2)}, u32[]{:S(2)}) collective-permute-start(bf16[2,8,7168]{2,1,0:T(8,128)(2,1)S(1)} %get-tuple-element.48), channel_id=1, source_target_pairs={{0,1},{1,0},{2,3},{3,2},{4,5},{5,4},{6,7},{7,6},{8,9},{9,8},{10,11... | collective-permute-start | bytes 688136 | tf_op jit(solution)/shard_map/ppermute | solution.py:222
  39.7 6.0 %collective-permute-start.9 = (bf16[8,7168]{1,0:T(8,128)(2,1)S(1)}, bf16[8,7168]{1,0:T(8,128)(2,1)S(1)}, u32[]{:S(2)}, u32[]{:S(2)}) collective-permute-start(bf16[8,7168]{1,0:T(8,128)(2,1)S(1)} %slice_bitcast_fusion.14), channel_id=1, source_target_pairs={{0,2},{1,3},{2,0},{3,1},{4,6},{5,7},{6,4},{7,5},{8,10},{9,11},{10,... | collective-permute-start | bytes 344072 | tf_op jit(solution)/shard_map/ppermute | solution.py:222
  41.5 6.7 %collective-permute-start.12 = (bf16[8,7168]{1,0:T(8,128)(2,1)S(1)}, bf16[8,7168]{1,0:T(8,128)(2,1)S(1)}, u32[]{:S(2)}, u32[]{:S(2)}) collective-permute-start(bf16[8,7168]{1,0:T(8,128)(2,1)S(1)} %slice_bitcast_fusion.12), channel_id=1, source_target_pairs={{0,2},{1,3},{2,0},{3,1},{4,6},{5,7},{6,4},{7,5},{8,10},{9,11},{10,... | collective-permute-start | bytes 344072 | tf_op jit(solution)/shard_map/ppermute | solution.py:222
  41.9 8.8 %collective-permute-start.15 = (bf16[8,7168]{1,0:T(8,128)(2,1)S(1)}, bf16[8,7168]{1,0:T(8,128)(2,1)S(1)}, u32[]{:S(2)}, u32[]{:S(2)}) collective-permute-start(bf16[8,7168]{1,0:T(8,128)(2,1)S(1)} %slice_bitcast_fusion.10), channel_id=1, source_target_pairs={{0,2},{1,3},{2,0},{3,1},{4,6},{5,7},{6,4},{7,5},{8,10},{9,11},{10,... | collective-permute-start | bytes 344072 | tf_op jit(solution)/shard_map/ppermute | solution.py:222
  43.7 8.9 %collective-permute-start.18 = (bf16[8,7168]{1,0:T(8,128)(2,1)S(1)}, bf16[8,7168]{1,0:T(8,128)(2,1)S(1)}, u32[]{:S(2)}, u32[]{:S(2)}) collective-permute-start(bf16[8,7168]{1,0:T(8,128)(2,1)S(1)} %slice_bitcast_fusion.8), channel_id=1, source_target_pairs={{0,2},{1,3},{2,0},{3,1},{4,6},{5,7},{6,4},{7,5},{8,10},{9,11},{10,... | collective-permute-start | bytes 344072 | tf_op jit(solution)/shard_map/ppermute | solution.py:222
  45.8 7.3 %collective-permute-start.10 = (bf16[8,7168]{1,0:T(8,128)(2,1)S(1)}, bf16[8,7168]{1,0:T(8,128)(2,1)S(1)}, u32[]{:S(2)}, u32[]{:S(2)}) collective-permute-start(bf16[8,7168]{1,0:T(8,128)(2,1)S(1)} %fusion.7), channel_id=1, source_target_pairs={{0,12},{4,8},{8,4},{12,0},{1,13},{5,9},{9,5},{13,1},{2,14},{6,10},... | collective-permute-start | bytes 344072 | tf_op jit(solution)/shard_map/ppermute | solution.py:221
  48.3 6.9 %collective-permute-start.13 = (bf16[8,7168]{1,0:T(8,128)(2,1)S(1)}, bf16[8,7168]{1,0:T(8,128)(2,1)S(1)}, u32[]{:S(2)}, u32[]{:S(2)}) collective-permute-start(bf16[8,7168]{1,0:T(8,128)(2,1)S(1)} %fusion.6), channel_id=1, source_target_pairs={{0,4},{4,0},{8,12},{12,8},{1,5},{5,1},{9,13},{13,9},{2,6},{6,2},{1... | collective-permute-start | bytes 344072 | tf_op jit(solution)/shard_map/ppermute | solution.py:221
  50.7 7.8 %collective-permute-start.16 = (bf16[8,7168]{1,0:T(8,128)(2,1)S(1)}, bf16[8,7168]{1,0:T(8,128)(2,1)S(1)}, u32[]{:S(2)}, u32[]{:S(2)}) collective-permute-start(bf16[8,7168]{1,0:T(8,128)(2,1)S(1)} %fusion.5), channel_id=1, source_target_pairs={{0,8},{4,12},{8,0},{12,4},{1,9},{5,13},{9,1},{13,5},{2,10},{6,14},... | collective-permute-start | bytes 344072 | tf_op jit(solution)/shard_map/ppermute | solution.py:221

commit v3 on v2

--- a/solution.py
+++ b/solution.py
@@ -9,7 +9,6 @@
 
 EXP_GROUP = 4
 LANES = 128
-LOADS = 4
 BLOCK = 128
 VMEM = pl.BlockSpec(memory_space=pltpu.VMEM)
 HBM = pl.BlockSpec(memory_space=pltpu.HBM)
@@ -117,15 +116,19 @@
 
 
 def expert_kernel(slice_count, pieces, rows_ref, *refs):
-    gate_refs, refs = refs[:pieces], refs[pieces:]
+    gate_refs, refs = list(refs[:pieces]), refs[pieces:]
     (up_scale_ref, down_scale_ref, pair_hbm, down_hbm, out_ref,
-     up_ref, down_ref, hidden_ref, act_ref, up_sems, down_sems) = refs
+     last_ref, up_ref, down_ref, hidden_ref, act_ref, last_sem, up_sems, down_sems) = refs
+    gate_refs.append(last_ref)
     depth = pair_hbm.shape[0]
     half, width = down_hbm.shape
     tile, tile_out = tile_of(half), tile_of(width, 1024)
     steps, steps_out = half // tile, width // tile_out
     share = -(-steps_out // steps)
-    band = depth // pieces
+    band = last_ref.shape[0]
+    starts = [0]
+    for gate_ref in gate_refs:
+        starts.append(starts[-1] + gate_ref.shape[0])
 
     def up_copy(i):
         return pltpu.make_async_copy(
@@ -136,15 +139,20 @@
         cols = pl.ds(i * tile_out, tile_out)
         return pltpu.make_async_copy(down_hbm.at[:, cols], down_ref.at[:, cols], down_sems.at[i])
 
-    for i in range(steps):
-        up_copy(i).start()
+    last_copy = pltpu.make_async_copy(pair_hbm.at[pl.ds(depth - band, band), pl.ds(0, half)], last_ref, last_sem)
+    last_copy.start()
     for i in range(steps):
         cols = pl.ds(i * tile, tile)
         total = None
-        for p in range(pieces):
-            scales = up_scale_ref[p * band // BLOCK : (p + 1) * band // BLOCK, cols]
+        for p in range(pieces + 1):
+            if i == 0 and p == pieces:
+                last_copy.wait()
+            if p == 1:
+                up_copy(i).start()
+            first, end = starts[p], starts[p + 1]
+            scales = up_scale_ref[first // BLOCK : end // BLOCK, cols]
             part = jnp.dot(
-                rows_ref[:, p * band : (p + 1) * band],
+                rows_ref[:, first:end],
                 scaled(gate_refs[p][:, cols], scales),
                 preferred_element_type=jnp.float32,
             )
@@ -177,17 +185,20 @@
     half, width = down.shape
     depth = pair.shape[0]
     pieces = len(gates)
-    held = 2 * (depth * half + half * width + 3 * count * half)
+    band = depth - sum(g.shape[0] for g in gates)
+    held = 2 * (band * half + depth * half + half * width + 3 * count * half)
     return pl.pallas_call(
         functools.partial(expert_kernel, slice_count, pieces),
         out_shape=pltpu.VMEM((count, width), jnp.bfloat16),
         in_specs=[VMEM] * (pieces + 3) + [HBM, HBM],
         out_specs=VMEM,
         scratch_shapes=[
+            pltpu.VMEM((band, half), jnp.bfloat16),
             pltpu.VMEM((depth, half), jnp.bfloat16),
             pltpu.VMEM((half, width), jnp.bfloat16),
             pltpu.VMEM((count, half), jnp.float32),
             pltpu.VMEM((count, half), jnp.bfloat16),
+            pltpu.SemaphoreType.DMA,
             pltpu.SemaphoreType.DMA((half // tile_of(half),)),
             pltpu.SemaphoreType.DMA((width // tile_of(width, 1024),)),
         ],
@@ -224,34 +235,41 @@
 
     pair, down = w_gate_up[0], w_down[0]
     up_scale, down_scale = spread_scales(gate_up_scales[0].T, down_scales[0])
-    band = pair.shape[0] // LOADS
-    load = lambda source, i: load_rows(source, i * band, band, down.shape[0])
-    gates = [load(pair, 0)] + [None] * (LOADS - 1)
+    blocks = pair.shape[0] // BLOCK
+    first, second = blocks // 4 * BLOCK, blocks * 3 // 8 * BLOCK
 
     packed = pack_rows(tokens, expert_ids, gate_weights)
     from_node = [packed] + [None] * (node_count - 1)
     for dz in range(node_count - 1, 0, -1):
         from_node[dz] = over_node(packed, dz)
-    group = [node_count - 1] + list(range(1, node_count - 1)) + [0]
-    same_core = []
-    for i, dz in enumerate(group):
-        piece = from_node[dz]
-        if i == 0:
-            piece, gates[0] = lax.optimization_barrier((piece, gates[0]))
-        others = [over_local(piece, 2 * dx) for dx in range(1, chip_count)]
-        if i < LOADS - 2:
-            others, later = lax.optimization_barrier((others, pair))
-            gates[i + 1] = load(later, i + 1)
-        same_core += [piece, *others]
-    gates[-1] = load(pair, LOADS - 1)
-    same_core, gates[1:-1] = lax.optimization_barrier((same_core, gates[1:-1]))
-    same_core = jnp.concatenate(same_core, axis=0)
-    rows = jnp.concatenate([same_core, over_local(same_core, 1)], axis=0)
+    group = list(range(node_count - 1, -1, -1))
+    over_both = lambda v, dz, dx: lax.ppermute(
+        v, ("node", "local"), xor_pairs(node_count * local_count, dz * local_count + 2 * dx)
+    )
+    over_chips = lambda v: [over_local(v, 2 * dx) for dx in range(1, chip_count)]
+    own = over_chips(packed)
+    direct = [over_both(packed, 1, dx) for dx in range(1, chip_count)]
+    gates = [load_rows(pair, 0, first, down.shape[0])]
+    pieces, others = {}, {0: own, 1: direct}
+    for dz in group:
+        pieces[dz] = from_node[dz]
+        if dz == node_count - 1:
+            pieces[dz], gates[0] = lax.optimization_barrier((pieces[dz], gates[0]))
+        if dz > 1:
+            others[dz] = over_chips(pieces[dz])
+    others[1], later = lax.optimization_barrier((others[1], pair))
+    gates.append(load_rows(later, first, second, down.shape[0]))
+    others, gates[1] = lax.optimization_barrier((others, gates[1]))
+    same_core = [jnp.concatenate([pieces[dz], *others[dz]], axis=0) for dz in group]
+    rows = jnp.concatenate(same_core + [over_local(v, 1) for v in same_core], axis=0)
     outputs = expert_apply(slice_count, rows, gates, up_scale, down_scale, pair, down)
     outputs = outputs.reshape(2, node_count, chip_count, row_count, width)
     returned = []
     for i, dz in enumerate(group):
         chip_sum = add(outputs[0, i], over_local(outputs[1, i], 1)).astype(jnp.bfloat16)
+        if dz == 1:
+            returned += [over_both(chip_sum[dx], dz, dx) for dx in range(chip_count)]
+            continue
         partial = chip_sum[0].astype(jnp.float32)
         for dx in range(1, chip_count):
             partial = partial + over_local(chip_sum[dx], 2 * dx).astype(jnp.float32)

time: 59.5 us -> 57.7 us (0.970)
  Pallas kernels: 20.9 us -> 17.8 us
  starting transfers between devices: 21.1 us -> 23.7 us
  waiting for transfers between devices: 15.7 us -> 14.4 us
    ppermute x0 -> x3, starting transfers between devices: none -> 4.73 us  [shards(): lax.ppermute(v, ('node', 'local'), xor_pairs(node_count * local_count, dz...]
    pallas_call x4 -> x2, Pallas kernels: 8.19 us -> 4.65 us  [load_rows(): pl.pallas_call(functools.partial(load_kernel, start), out_shape=pltpu.VME...]
    ppermute x13 -> x14, starting transfers between devices: 10.7 us -> 8.48 us  [shards(): lax.ppermute(v, 'local', xor_pairs(local_count, d))]
    ppermute x6 -> x5, waiting for transfers between devices: 9.38 us -> 8.18 us  [shards(): over_node = lambda v, d: lax.ppermute(v, 'node', xor_pairs(node_count, d))]
    ppermute x6 -> x5, starting transfers between devices: 10.4 us -> 10.5 us  [shards(): over_node = lambda v, d: lax.ppermute(v, 'node', xor_pairs(node_count, d))]
    ppermute x13 -> x14, waiting for transfers between devices: 6.29 us -> 6.25 us  [shards(): lax.ppermute(v, 'local', xor_pairs(local_count, d))]
  transfers between devices with their start and end apart: 19 -> 22, of which waited for: 16 -> 15; matrix products, arithmetic and copies ran while one was open for 0% -> 0% of each run, Pallas kernels for 14% -> 9%
where the time goes in v3:
time: 57.7 us; the launch traced here: 57.5 us
  starting transfers between devices  23.7 us (41%)
  Pallas kernels  17.8 us (31%)
  waiting for transfers between devices  14.4 us (25%)
  other arithmetic  1.08 us (2%)
    pallas_call x1, Pallas kernels, expert_apply(): pl.pallas_call(functools.partial(expert_kernel, slice_count, pieces), out...  11.9 us
    ppermute x5, starting transfers between devices, shards(): over_node = lambda v, d: lax.ppermute(v, 'node', xor_pairs(node_count, d))  10.5 us
    ppermute x14, starting transfers between devices, shards(): lax.ppermute(v, 'local', xor_pairs(local_count, d))  8.48 us
    ppermute x5, waiting for transfers between devices, shards(): over_node = lambda v, d: lax.ppermute(v, 'node', xor_pairs(node_count, d))  8.18 us
    ppermute x14, waiting for transfers between devices, shards(): lax.ppermute(v, 'local', xor_pairs(local_count, d))  6.25 us
    ppermute x3, starting transfers between devices, shards(): lax.ppermute(v, ('node', 'local'), xor_pairs(node_count * local_count, dz...  4.73 us
    pallas_call x2, Pallas kernels, load_rows(): pl.pallas_call(functools.partial(load_kernel, start), out_shape=pltpu.VME...  4.65 us
  transfers between devices with their start and end apart: 22, of which 15 were waited for; matrix products, arithmetic and copies ran while one was open for 0% of the time, Pallas kernels for 9%

profile of v3, /device:TPU:0, one launch (start us, length us, event | category | flops | bytes accessed | tf_op | source)
XLA Modules:
  0.0 57.5 jit_solution(9360689075602528745)
XLA Ops:
  0.0 1.0 %shard_map.73 = bf16[8,7296]{1,0:T(8,128)(2,1)S(1)} custom-call(bf16[8,7168]{1,0:T(8,128)(2,1)} %tokens_hbm.1, s32[8,8]{1,0:T(8,128)} %ids_hbm.1, bf16[8,8]{1,0:T(8,128)(2,1)} %gates_hbm.1), custom_call_target="tpu_custom_call" | custom-call | tf_op jit(solution)/shard_map/pallas_call | solution.py:41
  1.0 5.1 %collective-permute-start = (bf16[8,7296]{1,0:T(8,128)(2,1)S(1)}, bf16[8,7296]{1,0:T(8,128)(2,1)S(1)}, u32[]{:S(2)}, u32[]{:S(2)}) collective-permute-start(bf16[8,7296]{1,0:T(8,128)(2,1)S(1)} %shard_map.73), channel_id=1, source_target_pairs={{0,12},{4,8},{8,4},{12,0},{1,13},{5,9},{9,5},{13,1},{2,14},{6,10},... | collective-permute-start | bytes 350216 | tf_op jit(solution)/shard_map/ppermute | solution.py:232
  6.1 1.7 %collective-permute-start.2 = (bf16[8,7296]{1,0:T(8,128)(2,1)S(1)}, bf16[8,7296]{1,0:T(8,128)(2,1)S(1)}, u32[]{:S(2)}, u32[]{:S(2)}) collective-permute-start(bf16[8,7296]{1,0:T(8,128)(2,1)S(1)} %shard_map.73), channel_id=1, source_target_pairs={{0,6},{1,7},{2,4},{3,5},{4,2},{5,3},{6,0},{7,1},{8,14},{9,15},{10,... | collective-permute-start | bytes 350216 | tf_op jit(solution)/shard_map/ppermute | solution.py:246
  8.2 1.4 %collective-permute-start.6 = (bf16[8,7296]{1,0:T(8,128)(2,1)S(1)}, bf16[8,7296]{1,0:T(8,128)(2,1)S(1)}, u32[]{:S(2)}, u32[]{:S(2)}) collective-permute-start(bf16[8,7296]{1,0:T(8,128)(2,1)S(1)} %shard_map.73), channel_id=1, source_target_pairs={{0,4},{4,0},{8,12},{12,8},{1,5},{5,1},{9,13},{13,9},{2,6},{6,2},{1... | collective-permute-start | bytes 350216 | tf_op jit(solution)/shard_map/ppermute | solution.py:232
  9.6 2.1 %shard_map.74.refs_0_ = bf16[1792,1024]{1,0:T(8,128)(2,1)S(1)} custom-call(bf16[7168,2048]{1,0:T(8,128)(2,1)} %bitcast.64), custom_call_target="tpu_custom_call" | custom-call | bytes 3670016 | tf_op jit(solution)/shard_map/pallas_call | solution.py:101
  12.0 1.6 %collective-permute-start.5 = (bf16[8,7296]{1,0:T(8,128)(2,1)S(1)}, bf16[8,7296]{1,0:T(8,128)(2,1)S(1)}, u32[]{:S(2)}, u32[]{:S(2)}) collective-permute-start(bf16[8,7296]{1,0:T(8,128)(2,1)S(1)} %collective-permute-done), channel_id=1, source_target_pairs={{0,2},{1,3},{2,0},{3,1},{4,6},{5,7},{6,4},{7,5},{8,10},{9,11},{10,... | collective-permute-start | bytes 350216 | tf_op jit(solution)/shard_map/ppermute | solution.py:233
  13.6 2.5 %collective-permute-done.3 = bf16[8,7296]{1,0:T(8,128)(2,1)S(1)} collective-permute-done((bf16[8,7296]{1,0:T(8,128)(2,1)S(1)}, bf16[8,7296]{1,0:T(8,128)(2,1)S(1)}, u32[]{:S(2)}, u32[]{:S(2)}) %collective-permute-start.3) | collective-permute-done | bytes 116768 | tf_op jit(solution)/shard_map/ppermute | solution.py:232
  16.0 1.5 %collective-permute-start.4 = (bf16[8,7296]{1,0:T(8,128)(2,1)S(1)}, bf16[8,7296]{1,0:T(8,128)(2,1)S(1)}, u32[]{:S(2)}, u32[]{:S(2)}) collective-permute-start(bf16[8,7296]{1,0:T(8,128)(2,1)S(1)} %collective-permute-done.3), channel_id=1, source_target_pairs={{0,2},{1,3},{2,0},{3,1},{4,6},{5,7},{6,4},{7,5},{8,10},{9,11},{10,... | collective-permute-start | bytes 350216 | tf_op jit(solution)/shard_map/ppermute | solution.py:233
  17.5 2.6 %shard_map.75.refs_1_ = bf16[2688,1024]{1,0:T(8,128)(2,1)S(1)} custom-call(bf16[7168,2048]{1,0:T(8,128)(2,1)} %bitcast.65), custom_call_target="tpu_custom_call" | custom-call | bytes 5505024 | tf_op jit(solution)/shard_map/pallas_call | solution.py:101
  20.1 0.7 %collective-permute-done.4 = bf16[8,7296]{1,0:T(8,128)(2,1)S(1)} collective-permute-done((bf16[8,7296]{1,0:T(8,128)(2,1)S(1)}, bf16[8,7296]{1,0:T(8,128)(2,1)S(1)}, u32[]{:S(2)}, u32[]{:S(2)}) %collective-permute-start.4) | collective-permute-done | bytes 116768 | tf_op jit(solution)/shard_map/ppermute | solution.py:233
  21.1 0.6 collective-permute-start.8
  21.8 0.5 collective-permute-start.10
  23.6 11.9 %shard_map.77 = bf16[128,7168]{1,0:T(8,128)(2,1)S(1)} custom-call(bf16[128,7296]{1,0:T(8,128)(2,1)S(1)} %constant_dynamic-update-slice_fusion.rows_ref, bf16[1792,1024]{1,0:T(8,128)(2,1)S(1)} %shard_map.74.refs_0_, bf16[2688,1024]{1,0:T(8,128)(2,1)S(1)} %shard_map.75.refs_1_, bf16[56,2048]{1,0:T(8,128)(2,1)S(1)} %get-tuple-element.25.refs_2_, ...), custom_call_target="tpu_custom_call" | custom-call | flops 5637144576 | bytes 22020096 | tf_op jit(solution)/shard_map/pallas_call | solution.py:190
  38.3 1.6 %collective-permute-start.12 = (bf16[8,7168]{1,0:T(8,128)(2,1)S(1)}, bf16[8,7168]{1,0:T(8,128)(2,1)S(1)}, u32[]{:S(2)}, u32[]{:S(2)}) collective-permute-start(bf16[8,7168]{1,0:T(8,128)(2,1)S(1)} %slice_bitcast_fusion.14), channel_id=1, source_target_pairs={{0,2},{1,3},{2,0},{3,1},{4,6},{5,7},{6,4},{7,5},{8,10},{9,11},{10,... | collective-permute-start | bytes 344072 | tf_op jit(solution)/shard_map/ppermute | solution.py:233
  39.9 0.6 %collective-permute-start.15 = (bf16[8,7168]{1,0:T(8,128)(2,1)S(1)}, bf16[8,7168]{1,0:T(8,128)(2,1)S(1)}, u32[]{:S(2)}, u32[]{:S(2)}) collective-permute-start(bf16[8,7168]{1,0:T(8,128)(2,1)S(1)} %slice_bitcast_fusion.12), channel_id=1, source_target_pairs={{0,2},{1,3},{2,0},{3,1},{4,6},{5,7},{6,4},{7,5},{8,10},{9,11},{10,... | collective-permute-start | bytes 344072 | tf_op jit(solution)/shard_map/ppermute | solution.py:233
  40.5 1.2 %collective-permute-start.18 = (bf16[8,7168]{1,0:T(8,128)(2,1)S(1)}, bf16[8,7168]{1,0:T(8,128)(2,1)S(1)}, u32[]{:S(2)}, u32[]{:S(2)}) collective-permute-start(bf16[8,7168]{1,0:T(8,128)(2,1)S(1)} %get-tuple-element.35), channel_id=1, source_target_pairs={{0,4},{1,5},{2,6},{3,7},{4,0},{5,1},{6,2},{7,3},{8,12},{9,13},{10,... | collective-permute-start | bytes 344072 | tf_op jit(solution)/shard_map/ppermute | solution.py:246
  41.7 1.8 %collective-permute-start.19 = (bf16[8,7168]{1,0:T(8,128)(2,1)S(1)}, bf16[8,7168]{1,0:T(8,128)(2,1)S(1)}, u32[]{:S(2)}, u32[]{:S(2)}) collective-permute-start(bf16[8,7168]{1,0:T(8,128)(2,1)S(1)} %get-tuple-element.36), channel_id=1, source_target_pairs={{0,6},{1,7},{2,4},{3,5},{4,2},{5,3},{6,0},{7,1},{8,14},{9,15},{10,... | collective-permute-start | bytes 344072 | tf_op jit(solution)/shard_map/ppermute | solution.py:246
  43.6 0.6 %collective-permute-start.21 = (bf16[8,7168]{1,0:T(8,128)(2,1)S(1)}, bf16[8,7168]{1,0:T(8,128)(2,1)S(1)}, u32[]{:S(2)}, u32[]{:S(2)}) collective-permute-start(bf16[8,7168]{1,0:T(8,128)(2,1)S(1)} %slice_bitcast_fusion.8), channel_id=1, source_target_pairs={{0,2},{1,3},{2,0},{3,1},{4,6},{5,7},{6,4},{7,5},{8,10},{9,11},{10,... | collective-permute-start | bytes 344072 | tf_op jit(solution)/shard_map/ppermute | solution.py:233
  44.4 2.5 %collective-permute-start.13 = (bf16[8,7168]{1,0:T(8,128)(2,1)S(1)}, bf16[8,7168]{1,0:T(8,128)(2,1)S(1)}, u32[]{:S(2)}, u32[]{:S(2)}) collective-permute-start(bf16[8,7168]{1,0:T(8,128)(2,1)S(1)} %fusion.6), channel_id=1, source_target_pairs={{0,12},{4,8},{8,4},{12,0},{1,13},{5,9},{9,5},{13,1},{2,14},{6,10},... | collective-permute-start | bytes 344072 | tf_op jit(solution)/shard_map/ppermute | solution.py:232
  46.9 2.4 %collective-permute-done.15 = bf16[8,7168]{1,0:T(8,128)(2,1)S(1)} collective-permute-done((bf16[8,7168]{1,0:T(8,128)(2,1)S(1)}, bf16[8,7168]{1,0:T(8,128)(2,1)S(1)}, u32[]{:S(2)}, u32[]{:S(2)}) %collective-permute-start.15) | collective-permute-done | bytes 114720 | tf_op jit(solution)/shard_map/ppermute | solution.py:233
  49.3 1.5 %collective-permute-start.16 = (bf16[8,7168]{1,0:T(8,128)(2,1)S(1)}, bf16[8,7168]{1,0:T(8,128)(2,1)S(1)}, u32[]{:S(2)}, u32[]{:S(2)}) collective-permute-start(bf16[8,7168]{1,0:T(8,128)(2,1)S(1)} %fusion.5), channel_id=1, source_target_pairs={{0,8},{4,12},{8,0},{12,4},{1,9},{5,13},{9,1},{13,5},{2,10},{6,14},... | collective-permute-start | bytes 344072 | tf_op jit(solution)/shard_map/ppermute | solution.py:232
  51.1 0.8 %collective-permute-done.13 = bf16[8,7168]{1,0:T(8,128)(2,1)S(1)} collective-permute-done((bf16[8,7168]{1,0:T(8,128)(2,1)S(1)}, bf16[8,7168]{1,0:T(8,128)(2,1)S(1)}, u32[]{:S(2)}, u32[]{:S(2)}) %collective-permute-start.13) | collective-permute-done | bytes 114720 | tf_op jit(solution)/shard_map/ppermute | solution.py:232
  51.8 4.9 %collective-permute-done.16 = bf16[8,7168]{1,0:T(8,128)(2,1)S(1)} collective-permute-done((bf16[8,7168]{1,0:T(8,128)(2,1)S(1)}, bf16[8,7168]{1,0:T(8,128)(2,1)S(1)}, u32[]{:S(2)}, u32[]{:S(2)}) %collective-permute-start.16) | collective-permute-done | bytes 114720 | tf_op jit(solution)/shard_map/ppermute | solution.py:232
  56.8 0.7 %add_convert_fusion = bf16[8,7168]{1,0:T(8,128)(2,1)} fusion(bf16[8,7168]{1,0:T(8,128)(2,1)S(1)} %collective-permute-done.19, bf16[8,7168]{1,0:T(8,128)(2,1)S(1)} %collective-permute-done.18, bf16[8,7168]{1,0:T(8,128)(2,1)S(1)} %collective-permute-done.16, bf16[8,7168]{1,0:T(8,128)(2,1)S(1)} %collective-permute-done.13, ...), kind=kLoop, calls=%fused_computation.26 | loop fusion | flops 802816 | bytes 802816 | tf_op jit(solution)/shard_map/convert_element_type | solution.py:279
  (54 shorter events, 5.8 us)
Async XLA Ops:
  1.0 11.0 %collective-permute-start = (bf16[8,7296]{1,0:T(8,128)(2,1)S(1)}, bf16[8,7296]{1,0:T(8,128)(2,1)S(1)}, u32[]{:S(2)}, u32[]{:S(2)}) collective-permute-start(bf16[8,7296]{1,0:T(8,128)(2,1)S(1)} %shard_map.73), channel_id=1, source_target_pairs={{0,12},{4,8},{8,4},{12,0},{1,13},{5,9},{9,5},{13,1},{2,14},{6,10},... | collective-permute-start | bytes 350216 | tf_op jit(solution)/shard_map/ppermute | solution.py:232
  6.1 9.9 %collective-permute-start.3 = (bf16[8,7296]{1,0:T(8,128)(2,1)S(1)}, bf16[8,7296]{1,0:T(8,128)(2,1)S(1)}, u32[]{:S(2)}, u32[]{:S(2)}) collective-permute-start(bf16[8,7296]{1,0:T(8,128)(2,1)S(1)} %shard_map.73), channel_id=1, source_target_pairs={{0,8},{4,12},{8,0},{12,4},{1,9},{5,13},{9,1},{13,5},{2,10},{6,14},... | collective-permute-start | bytes 350216 | tf_op jit(solution)/shard_map/ppermute | solution.py:232
  6.1 11.5 %collective-permute-start.2 = (bf16[8,7296]{1,0:T(8,128)(2,1)S(1)}, bf16[8,7296]{1,0:T(8,128)(2,1)S(1)}, u32[]{:S(2)}, u32[]{:S(2)}) collective-permute-start(bf16[8,7296]{1,0:T(8,128)(2,1)S(1)} %shard_map.73), channel_id=1, source_target_pairs={{0,6},{1,7},{2,4},{3,5},{4,2},{5,3},{6,0},{7,1},{8,14},{9,15},{10,... | collective-permute-start | bytes 350216 | tf_op jit(solution)/shard_map/ppermute | solution.py:246
  7.8 12.3 %collective-permute-start.1 = (bf16[8,7296]{1,0:T(8,128)(2,1)S(1)}, bf16[8,7296]{1,0:T(8,128)(2,1)S(1)}, u32[]{:S(2)}, u32[]{:S(2)}) collective-permute-start(bf16[8,7296]{1,0:T(8,128)(2,1)S(1)} %shard_map.73), channel_id=1, source_target_pairs={{0,2},{1,3},{2,0},{3,1},{4,6},{5,7},{6,4},{7,5},{8,10},{9,11},{10,... | collective-permute-start | bytes 350216 | tf_op jit(solution)/shard_map/ppermute | solution.py:233
  8.2 12.7 %collective-permute-start.6 = (bf16[8,7296]{1,0:T(8,128)(2,1)S(1)}, bf16[8,7296]{1,0:T(8,128)(2,1)S(1)}, u32[]{:S(2)}, u32[]{:S(2)}) collective-permute-start(bf16[8,7296]{1,0:T(8,128)(2,1)S(1)} %shard_map.73), channel_id=1, source_target_pairs={{0,4},{4,0},{8,12},{12,8},{1,5},{5,1},{9,13},{13,9},{2,6},{6,2},{1... | collective-permute-start | bytes 350216 | tf_op jit(solution)/shard_map/ppermute | solution.py:232
  9.6 2.1 %copy-start = (f32[1,56,16]{1,2,0:T(8,128)S(1)}, f32[1,56,16]{1,2,0:T(8,128)}, u32[]{:S(2)}) copy-start(f32[1,56,16]{1,2,0:T(8,128)} %param.11) | copy-start | bytes 10756
  9.6 2.1 %copy-start.1 = (f32[1,8,56]{2,1,0:T(8,128)S(1)}, f32[1,8,56]{2,1,0:T(8,128)}, u32[]{:S(2)}) copy-start(f32[1,8,56]{2,1,0:T(8,128)} %param.13) | copy-start | bytes 5380
  12.0 8.1 %collective-permute-start.5 = (bf16[8,7296]{1,0:T(8,128)(2,1)S(1)}, bf16[8,7296]{1,0:T(8,128)(2,1)S(1)}, u32[]{:S(2)}, u32[]{:S(2)}) collective-permute-start(bf16[8,7296]{1,0:T(8,128)(2,1)S(1)} %collective-permute-done), channel_id=1, source_target_pairs={{0,2},{1,3},{2,0},{3,1},{4,6},{5,7},{6,4},{7,5},{8,10},{9,11},{10,... | collective-permute-start | bytes 350216 | tf_op jit(solution)/shard_map/ppermute | solution.py:233
  16.0 4.8 %collective-permute-start.4 = (bf16[8,7296]{1,0:T(8,128)(2,1)S(1)}, bf16[8,7296]{1,0:T(8,128)(2,1)S(1)}, u32[]{:S(2)}, u32[]{:S(2)}) collective-permute-start(bf16[8,7296]{1,0:T(8,128)(2,1)S(1)} %collective-permute-done.3), channel_id=1, source_target_pairs={{0,2},{1,3},{2,0},{3,1},{4,6},{5,7},{6,4},{7,5},{8,10},{9,11},{10,... | collective-permute-start | bytes 350216 | tf_op jit(solution)/shard_map/ppermute | solution.py:233
  21.0 1.6 %collective-permute-start.7 = (bf16[16,7296]{1,0:T(8,128)(2,1)S(1)}, bf16[16,7296]{1,0:T(8,128)(2,1)S(1)}, u32[]{:S(2)}, u32[]{:S(2)}) collective-permute-start(bf16[16,7296]{1,0:T(8,128)(2,1)S(1)} %pad_maximum_fusion), channel_id=1, source_target_pairs={{0,1},{1,0},{2,3},{3,2},{4,5},{5,4},{6,7},{7,6},{8,9},{9,8},{10,11... | collective-permute-start | bytes 700424 | tf_op jit(solution)/shard_map/ppermute | solution.py:233
  21.1 1.8 %collective-permute-start.8 = (bf16[16,7296]{1,0:T(8,128)(2,1)S(1)}, bf16[16,7296]{1,0:T(8,128)(2,1)S(1)}, u32[]{:S(2)}, u32[]{:S(2)}) collective-permute-start(bf16[16,7296]{1,0:T(8,128)(2,1)S(1)} %pad_maximum_fusion.1), channel_id=1, source_target_pairs={{0,1},{1,0},{2,3},{3,2},{4,5},{5,4},{6,7},{7,6},{8,9},{9,8},{10,11... | collective-permute-start | bytes 700424 | tf_op jit(solution)/shard_map/ppermute | solution.py:233
  21.7 1.6 %collective-permute-start.9 = (bf16[16,7296]{1,0:T(8,128)(2,1)S(1)}, bf16[16,7296]{1,0:T(8,128)(2,1)S(1)}, u32[]{:S(2)}, u32[]{:S(2)}) collective-permute-start(bf16[16,7296]{1,0:T(8,128)(2,1)S(1)} %pad_maximum_fusion.2), channel_id=1, source_target_pairs={{0,1},{1,0},{2,3},{3,2},{4,5},{5,4},{6,7},{7,6},{8,9},{9,8},{10,11... | collective-permute-start | bytes 700424 | tf_op jit(solution)/shard_map/ppermute | solution.py:233
  21.8 1.8 %collective-permute-start.10 = (bf16[16,7296]{1,0:T(8,128)(2,1)S(1)}, bf16[16,7296]{1,0:T(8,128)(2,1)S(1)}, u32[]{:S(2)}, u32[]{:S(2)}) collective-permute-start(bf16[16,7296]{1,0:T(8,128)(2,1)S(1)} %pad_maximum_fusion.3), channel_id=1, source_target_pairs={{0,1},{1,0},{2,3},{3,2},{4,5},{5,4},{6,7},{7,6},{8,9},{9,8},{10,11... | collective-permute-start | bytes 700424 | tf_op jit(solution)/shard_map/ppermute | solution.py:233
  35.6 1.6 %collective-permute-start.11 = (bf16[2,8,7168]{2,1,0:T(8,128)(2,1)S(1)}, bf16[2,8,7168]{2,1,0:T(8,128)(2,1)S(1)}, u32[]{:S(2)}, u32[]{:S(2)}) collective-permute-start(bf16[2,8,7168]{2,1,0:T(8,128)(2,1)S(1)} %get-tuple-element.34), channel_id=1, source_target_pairs={{0,1},{1,0},{2,3},{3,2},{4,5},{5,4},{6,7},{7,6},{8,9},{9,8},{10,11... | collective-permute-start | bytes 688136 | tf_op jit(solution)/shard_map/ppermute | solution.py:233
  35.9 1.6 %collective-permute-start.14 = (bf16[2,8,7168]{2,1,0:T(8,128)(2,1)S(1)}, bf16[2,8,7168]{2,1,0:T(8,128)(2,1)S(1)}, u32[]{:S(2)}, u32[]{:S(2)}) collective-permute-start(bf16[2,8,7168]{2,1,0:T(8,128)(2,1)S(1)} %get-tuple-element.33), channel_id=1, source_target_pairs={{0,1},{1,0},{2,3},{3,2},{4,5},{5,4},{6,7},{7,6},{8,9},{9,8},{10,11... | collective-permute-start | bytes 688136 | tf_op jit(solution)/shard_map/ppermute | solution.py:233
  36.1 1.6 %collective-permute-start.17 = (bf16[2,8,7168]{2,1,0:T(8,128)(2,1)S(1)}, bf16[2,8,7168]{2,1,0:T(8,128)(2,1)S(1)}, u32[]{:S(2)}, u32[]{:S(2)}) collective-permute-start(bf16[2,8,7168]{2,1,0:T(8,128)(2,1)S(1)} %get-tuple-element.32), channel_id=1, source_target_pairs={{0,1},{1,0},{2,3},{3,2},{4,5},{5,4},{6,7},{7,6},{8,9},{9,8},{10,11... | collective-permute-start | bytes 688136 | tf_op jit(solution)/shard_map/ppermute | solution.py:233
  36.4 1.7 %collective-permute-start.20 = (bf16[2,8,7168]{2,1,0:T(8,128)(2,1)S(1)}, bf16[2,8,7168]{2,1,0:T(8,128)(2,1)S(1)}, u32[]{:S(2)}, u32[]{:S(2)}) collective-permute-start(bf16[2,8,7168]{2,1,0:T(8,128)(2,1)S(1)} %get-tuple-element.31), channel_id=1, source_target_pairs={{0,1},{1,0},{2,3},{3,2},{4,5},{5,4},{6,7},{7,6},{8,9},{9,8},{10,11... | collective-permute-start | bytes 688136 | tf_op jit(solution)/shard_map/ppermute | solution.py:233
  38.3 6.0 %collective-permute-start.12 = (bf16[8,7168]{1,0:T(8,128)(2,1)S(1)}, bf16[8,7168]{1,0:T(8,128)(2,1)S(1)}, u32[]{:S(2)}, u32[]{:S(2)}) collective-permute-start(bf16[8,7168]{1,0:T(8,128)(2,1)S(1)} %slice_bitcast_fusion.14), channel_id=1, source_target_pairs={{0,2},{1,3},{2,0},{3,1},{4,6},{5,7},{6,4},{7,5},{8,10},{9,11},{10,... | collective-permute-start | bytes 344072 | tf_op jit(solution)/shard_map/ppermute | solution.py:233
  39.9 9.4 %collective-permute-start.15 = (bf16[8,7168]{1,0:T(8,128)(2,1)S(1)}, bf16[8,7168]{1,0:T(8,128)(2,1)S(1)}, u32[]{:S(2)}, u32[]{:S(2)}) collective-permute-start(bf16[8,7168]{1,0:T(8,128)(2,1)S(1)} %slice_bitcast_fusion.12), channel_id=1, source_target_pairs={{0,2},{1,3},{2,0},{3,1},{4,6},{5,7},{6,4},{7,5},{8,10},{9,11},{10,... | collective-permute-start | bytes 344072 | tf_op jit(solution)/shard_map/ppermute | solution.py:233
  40.5 10.3 %collective-permute-start.18 = (bf16[8,7168]{1,0:T(8,128)(2,1)S(1)}, bf16[8,7168]{1,0:T(8,128)(2,1)S(1)}, u32[]{:S(2)}, u32[]{:S(2)}) collective-permute-start(bf16[8,7168]{1,0:T(8,128)(2,1)S(1)} %get-tuple-element.35), channel_id=1, source_target_pairs={{0,4},{1,5},{2,6},{3,7},{4,0},{5,1},{6,2},{7,3},{8,12},{9,13},{10,... | collective-permute-start | bytes 344072 | tf_op jit(solution)/shard_map/ppermute | solution.py:246
  41.7 9.1 %collective-permute-start.19 = (bf16[8,7168]{1,0:T(8,128)(2,1)S(1)}, bf16[8,7168]{1,0:T(8,128)(2,1)S(1)}, u32[]{:S(2)}, u32[]{:S(2)}) collective-permute-start(bf16[8,7168]{1,0:T(8,128)(2,1)S(1)} %get-tuple-element.36), channel_id=1, source_target_pairs={{0,6},{1,7},{2,4},{3,5},{4,2},{5,3},{6,0},{7,1},{8,14},{9,15},{10,... | collective-permute-start | bytes 344072 | tf_op jit(solution)/shard_map/ppermute | solution.py:246
  43.6 7.5 %collective-permute-start.21 = (bf16[8,7168]{1,0:T(8,128)(2,1)S(1)}, bf16[8,7168]{1,0:T(8,128)(2,1)S(1)}, u32[]{:S(2)}, u32[]{:S(2)}) collective-permute-start(bf16[8,7168]{1,0:T(8,128)(2,1)S(1)} %slice_bitcast_fusion.8), channel_id=1, source_target_pairs={{0,2},{1,3},{2,0},{3,1},{4,6},{5,7},{6,4},{7,5},{8,10},{9,11},{10,... | collective-permute-start | bytes 344072 | tf_op jit(solution)/shard_map/ppermute | solution.py:233
  44.4 7.4 %collective-permute-start.13 = (bf16[8,7168]{1,0:T(8,128)(2,1)S(1)}, bf16[8,7168]{1,0:T(8,128)(2,1)S(1)}, u32[]{:S(2)}, u32[]{:S(2)}) collective-permute-start(bf16[8,7168]{1,0:T(8,128)(2,1)S(1)} %fusion.6), channel_id=1, source_target_pairs={{0,12},{4,8},{8,4},{12,0},{1,13},{5,9},{9,5},{13,1},{2,14},{6,10},... | collective-permute-start | bytes 344072 | tf_op jit(solution)/shard_map/ppermute | solution.py:232
  49.3 7.5 %collective-permute-start.16 = (bf16[8,7168]{1,0:T(8,128)(2,1)S(1)}, bf16[8,7168]{1,0:T(8,128)(2,1)S(1)}, u32[]{:S(2)}, u32[]{:S(2)}) collective-permute-start(bf16[8,7168]{1,0:T(8,128)(2,1)S(1)} %fusion.5), channel_id=1, source_target_pairs={{0,8},{4,12},{8,0},{12,4},{1,9},{5,13},{9,1},{13,5},{2,10},{6,14},... | collective-permute-start | bytes 344072 | tf_op jit(solution)/shard_map/ppermute | solution.py:232

commit v4 on v3

--- a/solution.py
+++ b/solution.py
@@ -236,7 +236,7 @@
     pair, down = w_gate_up[0], w_down[0]
     up_scale, down_scale = spread_scales(gate_up_scales[0].T, down_scales[0])
     blocks = pair.shape[0] // BLOCK
-    first, second = blocks // 4 * BLOCK, blocks * 3 // 8 * BLOCK
+    first, second = blocks * 3 // 8 * BLOCK, blocks // 2 * BLOCK
 
     packed = pack_rows(tokens, expert_ids, gate_weights)
     from_node = [packed] + [None] * (node_count - 1)
@@ -264,17 +264,22 @@
     rows = jnp.concatenate(same_core + [over_local(v, 1) for v in same_core], axis=0)
     outputs = expert_apply(slice_count, rows, gates, up_scale, down_scale, pair, down)
     outputs = outputs.reshape(2, node_count, chip_count, row_count, width)
-    returned = []
+    sums = {}
     for i, dz in enumerate(group):
-        chip_sum = add(outputs[0, i], over_local(outputs[1, i], 1)).astype(jnp.bfloat16)
-        if dz == 1:
-            returned += [over_both(chip_sum[dx], dz, dx) for dx in range(chip_count)]
-            continue
-        partial = chip_sum[0].astype(jnp.float32)
-        for dx in range(1, chip_count):
-            partial = partial + over_local(chip_sum[dx], 2 * dx).astype(jnp.float32)
-        partial = partial.astype(jnp.bfloat16)
-        returned.append(over_node(partial, dz) if dz else partial)
+        sums[dz] = add(outputs[0, i], over_local(outputs[1, i], 1)).astype(jnp.bfloat16)
+
+    def group_sum(first, others):
+        total = first.astype(jnp.float32)
+        for other in others:
+            total = total + other.astype(jnp.float32)
+        return total.astype(jnp.bfloat16)
+
+    over_pieces = lambda v: [over_local(v[dx], 2 * dx) for dx in range(1, chip_count)]
+    far = range(node_count - 1, 1, -1)
+    arrived = {dz: over_pieces(sums[dz]) for dz in far}
+    returned = [over_node(group_sum(sums[dz][0], arrived[dz]), dz) for dz in far]
+    returned += [over_both(sums[1][dx], 1, dx) for dx in range(chip_count)]
+    returned.append(group_sum(sums[0][0], over_pieces(sums[0])))
     combined = functools.reduce(jnp.add, [v.astype(jnp.float32) for v in returned])
     return combined.astype(jnp.bfloat16)
 

time: 57.7 us -> 56.6 us (0.981)
  waiting for transfers between devices: 14.4 us -> 13.4 us
    pallas_call x1, Pallas kernels: 11.9 us -> 10.8 us  [expert_apply(): pl.pallas_call(functools.partial(expert_kernel, slice_count, pieces), out...]
    pallas_call x2, Pallas kernels: 4.65 us -> 5.69 us  [load_rows(): pl.pallas_call(functools.partial(load_kernel, start), out_shape=pltpu.VME...]
  transfers between devices with their start and end apart: 22 -> 22, of which waited for: 15 -> 15; matrix products, arithmetic and copies ran while one was open for 0% -> 0% of each run, Pallas kernels for 9% -> 11%
where the time goes in v4:
time: 56.6 us; the launch traced here: 56.5 us
  starting transfers between devices  23.7 us (42%)
  Pallas kernels  17.7 us (31%)
  waiting for transfers between devices  13.4 us (24%)
  other arithmetic  1.08 us (2%)
    pallas_call x1, Pallas kernels, expert_apply(): pl.pallas_call(functools.partial(expert_kernel, slice_count, pieces), out...  10.8 us
    ppermute x5, starting transfers between devices, shards(): over_node = lambda v, d: lax.ppermute(v, 'node', xor_pairs(node_count, d))  10.5 us
    ppermute x14, starting transfers between devices, shards(): lax.ppermute(v, 'local', xor_pairs(local_count, d))  8.48 us
    ppermute x5, waiting for transfers between devices, shards(): over_node = lambda v, d: lax.ppermute(v, 'node', xor_pairs(node_count, d))  7.66 us
    ppermute x14, waiting for transfers between devices, shards(): lax.ppermute(v, 'local', xor_pairs(local_count, d))  5.72 us
    pallas_call x2, Pallas kernels, load_rows(): pl.pallas_call(functools.partial(load_kernel, start), out_shape=pltpu.VME...  5.69 us
    ppermute x3, starting transfers between devices, shards(): lax.ppermute(v, ('node', 'local'), xor_pairs(node_count * local_count, dz...  4.73 us
  transfers between devices with their start and end apart: 22, of which 15 were waited for; matrix products, arithmetic and copies ran while one was open for 0% of the time, Pallas kernels for 11%

profile of v4, /device:TPU:0, one launch (start us, length us, event | category | flops | bytes accessed | tf_op | source)
XLA Modules:
  0.0 56.5 jit_solution(13276336756058631639)
XLA Ops:
  0.0 1.0 %shard_map.73 = bf16[8,7296]{1,0:T(8,128)(2,1)S(1)} custom-call(bf16[8,7168]{1,0:T(8,128)(2,1)} %tokens_hbm.1, s32[8,8]{1,0:T(8,128)} %ids_hbm.1, bf16[8,8]{1,0:T(8,128)(2,1)} %gates_hbm.1), custom_call_target="tpu_custom_call" | custom-call | tf_op jit(solution)/shard_map/pallas_call | solution.py:41
  1.0 5.1 %collective-permute-start = (bf16[8,7296]{1,0:T(8,128)(2,1)S(1)}, bf16[8,7296]{1,0:T(8,128)(2,1)S(1)}, u32[]{:S(2)}, u32[]{:S(2)}) collective-permute-start(bf16[8,7296]{1,0:T(8,128)(2,1)S(1)} %shard_map.73), channel_id=1, source_target_pairs={{0,12},{4,8},{8,4},{12,0},{1,13},{5,9},{9,5},{13,1},{2,14},{6,10},... | collective-permute-start | bytes 350216 | tf_op jit(solution)/shard_map/ppermute | solution.py:232
  6.1 1.7 %collective-permute-start.2 = (bf16[8,7296]{1,0:T(8,128)(2,1)S(1)}, bf16[8,7296]{1,0:T(8,128)(2,1)S(1)}, u32[]{:S(2)}, u32[]{:S(2)}) collective-permute-start(bf16[8,7296]{1,0:T(8,128)(2,1)S(1)} %shard_map.73), channel_id=1, source_target_pairs={{0,6},{1,7},{2,4},{3,5},{4,2},{5,3},{6,0},{7,1},{8,14},{9,15},{10,... | collective-permute-start | bytes 350216 | tf_op jit(solution)/shard_map/ppermute | solution.py:246
  8.2 1.4 %collective-permute-start.6 = (bf16[8,7296]{1,0:T(8,128)(2,1)S(1)}, bf16[8,7296]{1,0:T(8,128)(2,1)S(1)}, u32[]{:S(2)}, u32[]{:S(2)}) collective-permute-start(bf16[8,7296]{1,0:T(8,128)(2,1)S(1)} %shard_map.73), channel_id=1, source_target_pairs={{0,4},{4,0},{8,12},{12,8},{1,5},{5,1},{9,13},{13,9},{2,6},{6,2},{1... | collective-permute-start | bytes 350216 | tf_op jit(solution)/shard_map/ppermute | solution.py:232
  9.6 2.6 %shard_map.74.refs_0_ = bf16[2688,1024]{1,0:T(8,128)(2,1)S(1)} custom-call(bf16[7168,2048]{1,0:T(8,128)(2,1)} %bitcast.64), custom_call_target="tpu_custom_call" | custom-call | bytes 5505024 | tf_op jit(solution)/shard_map/pallas_call | solution.py:101
  12.5 1.6 %collective-permute-start.5 = (bf16[8,7296]{1,0:T(8,128)(2,1)S(1)}, bf16[8,7296]{1,0:T(8,128)(2,1)S(1)}, u32[]{:S(2)}, u32[]{:S(2)}) collective-permute-start(bf16[8,7296]{1,0:T(8,128)(2,1)S(1)} %collective-permute-done), channel_id=1, source_target_pairs={{0,2},{1,3},{2,0},{3,1},{4,6},{5,7},{6,4},{7,5},{8,10},{9,11},{10,... | collective-permute-start | bytes 350216 | tf_op jit(solution)/shard_map/ppermute | solution.py:233
  14.1 1.9 %collective-permute-done.3 = bf16[8,7296]{1,0:T(8,128)(2,1)S(1)} collective-permute-done((bf16[8,7296]{1,0:T(8,128)(2,1)S(1)}, bf16[8,7296]{1,0:T(8,128)(2,1)S(1)}, u32[]{:S(2)}, u32[]{:S(2)}) %collective-permute-start.3) | collective-permute-done | bytes 116768 | tf_op jit(solution)/shard_map/ppermute | solution.py:232
  16.0 1.5 %collective-permute-start.4 = (bf16[8,7296]{1,0:T(8,128)(2,1)S(1)}, bf16[8,7296]{1,0:T(8,128)(2,1)S(1)}, u32[]{:S(2)}, u32[]{:S(2)}) collective-permute-start(bf16[8,7296]{1,0:T(8,128)(2,1)S(1)} %collective-permute-done.3), channel_id=1, source_target_pairs={{0,2},{1,3},{2,0},{3,1},{4,6},{5,7},{6,4},{7,5},{8,10},{9,11},{10,... | collective-permute-start | bytes 350216 | tf_op jit(solution)/shard_map/ppermute | solution.py:233
  17.5 3.1 %shard_map.75.refs_1_ = bf16[3584,1024]{1,0:T(8,128)(2,1)S(1)} custom-call(bf16[7168,2048]{1,0:T(8,128)(2,1)} %bitcast.65), custom_call_target="tpu_custom_call" | custom-call | bytes 7340032 | tf_op jit(solution)/shard_map/pallas_call | solution.py:101
  21.1 0.6 collective-permute-start.8
  21.8 0.5 collective-permute-start.10
  23.6 10.8 %shard_map.77 = bf16[128,7168]{1,0:T(8,128)(2,1)S(1)} custom-call(bf16[128,7296]{1,0:T(8,128)(2,1)S(1)} %constant_dynamic-update-slice_fusion.rows_ref, bf16[2688,1024]{1,0:T(8,128)(2,1)S(1)} %shard_map.74.refs_0_, bf16[3584,1024]{1,0:T(8,128)(2,1)S(1)} %shard_map.75.refs_1_, bf16[56,2048]{1,0:T(8,128)(2,1)S(1)} %get-tuple-element.25.refs_2_, ...), custom_call_target="tpu_custom_call" | custom-call | flops 5637144576 | bytes 22020096 | tf_op jit(solution)/shard_map/pallas_call | solution.py:190
  35.6 0.5 collective-permute-done.11
  37.3 1.6 %collective-permute-start.12 = (bf16[8,7168]{1,0:T(8,128)(2,1)S(1)}, bf16[8,7168]{1,0:T(8,128)(2,1)S(1)}, u32[]{:S(2)}, u32[]{:S(2)}) collective-permute-start(bf16[8,7168]{1,0:T(8,128)(2,1)S(1)} %slice_bitcast_fusion.14), channel_id=1, source_target_pairs={{0,2},{1,3},{2,0},{3,1},{4,6},{5,7},{6,4},{7,5},{8,10},{9,11},{10,... | collective-permute-start | bytes 344072 | tf_op jit(solution)/shard_map/ppermute | solution.py:233
  38.8 0.6 %collective-permute-start.15 = (bf16[8,7168]{1,0:T(8,128)(2,1)S(1)}, bf16[8,7168]{1,0:T(8,128)(2,1)S(1)}, u32[]{:S(2)}, u32[]{:S(2)}) collective-permute-start(bf16[8,7168]{1,0:T(8,128)(2,1)S(1)} %slice_bitcast_fusion.12), channel_id=1, source_target_pairs={{0,2},{1,3},{2,0},{3,1},{4,6},{5,7},{6,4},{7,5},{8,10},{9,11},{10,... | collective-permute-start | bytes 344072 | tf_op jit(solution)/shard_map/ppermute | solution.py:233
  39.5 1.2 %collective-permute-start.18 = (bf16[8,7168]{1,0:T(8,128)(2,1)S(1)}, bf16[8,7168]{1,0:T(8,128)(2,1)S(1)}, u32[]{:S(2)}, u32[]{:S(2)}) collective-permute-start(bf16[8,7168]{1,0:T(8,128)(2,1)S(1)} %get-tuple-element.35), channel_id=1, source_target_pairs={{0,4},{1,5},{2,6},{3,7},{4,0},{5,1},{6,2},{7,3},{8,12},{9,13},{10,... | collective-permute-start | bytes 344072 | tf_op jit(solution)/shard_map/ppermute | solution.py:246
  40.7 1.8 %collective-permute-start.19 = (bf16[8,7168]{1,0:T(8,128)(2,1)S(1)}, bf16[8,7168]{1,0:T(8,128)(2,1)S(1)}, u32[]{:S(2)}, u32[]{:S(2)}) collective-permute-start(bf16[8,7168]{1,0:T(8,128)(2,1)S(1)} %get-tuple-element.36), channel_id=1, source_target_pairs={{0,6},{1,7},{2,4},{3,5},{4,2},{5,3},{6,0},{7,1},{8,14},{9,15},{10,... | collective-permute-start | bytes 344072 | tf_op jit(solution)/shard_map/ppermute | solution.py:246
  42.5 0.6 %collective-permute-start.21 = (bf16[8,7168]{1,0:T(8,128)(2,1)S(1)}, bf16[8,7168]{1,0:T(8,128)(2,1)S(1)}, u32[]{:S(2)}, u32[]{:S(2)}) collective-permute-start(bf16[8,7168]{1,0:T(8,128)(2,1)S(1)} %slice_bitcast_fusion.8), channel_id=1, source_target_pairs={{0,2},{1,3},{2,0},{3,1},{4,6},{5,7},{6,4},{7,5},{8,10},{9,11},{10,... | collective-permute-start | bytes 344072 | tf_op jit(solution)/shard_map/ppermute | solution.py:233
  43.3 2.5 %collective-permute-start.13 = (bf16[8,7168]{1,0:T(8,128)(2,1)S(1)}, bf16[8,7168]{1,0:T(8,128)(2,1)S(1)}, u32[]{:S(2)}, u32[]{:S(2)}) collective-permute-start(bf16[8,7168]{1,0:T(8,128)(2,1)S(1)} %fusion.6), channel_id=1, source_target_pairs={{0,12},{4,8},{8,4},{12,0},{1,13},{5,9},{9,5},{13,1},{2,14},{6,10},... | collective-permute-start | bytes 344072 | tf_op jit(solution)/shard_map/ppermute | solution.py:232
  45.8 2.4 %collective-permute-done.15 = bf16[8,7168]{1,0:T(8,128)(2,1)S(1)} collective-permute-done((bf16[8,7168]{1,0:T(8,128)(2,1)S(1)}, bf16[8,7168]{1,0:T(8,128)(2,1)S(1)}, u32[]{:S(2)}, u32[]{:S(2)}) %collective-permute-start.15) | collective-permute-done | bytes 114720 | tf_op jit(solution)/shard_map/ppermute | solution.py:233
  48.3 1.5 %collective-permute-start.16 = (bf16[8,7168]{1,0:T(8,128)(2,1)S(1)}, bf16[8,7168]{1,0:T(8,128)(2,1)S(1)}, u32[]{:S(2)}, u32[]{:S(2)}) collective-permute-start(bf16[8,7168]{1,0:T(8,128)(2,1)S(1)} %fusion.5), channel_id=1, source_target_pairs={{0,8},{4,12},{8,0},{12,4},{1,9},{5,13},{9,1},{13,5},{2,10},{6,14},... | collective-permute-start | bytes 344072 | tf_op jit(solution)/shard_map/ppermute | solution.py:232
  50.0 0.8 %collective-permute-done.13 = bf16[8,7168]{1,0:T(8,128)(2,1)S(1)} collective-permute-done((bf16[8,7168]{1,0:T(8,128)(2,1)S(1)}, bf16[8,7168]{1,0:T(8,128)(2,1)S(1)}, u32[]{:S(2)}, u32[]{:S(2)}) %collective-permute-start.13) | collective-permute-done | bytes 114720 | tf_op jit(solution)/shard_map/ppermute | solution.py:232
  50.8 4.9 %collective-permute-done.16 = bf16[8,7168]{1,0:T(8,128)(2,1)S(1)} collective-permute-done((bf16[8,7168]{1,0:T(8,128)(2,1)S(1)}, bf16[8,7168]{1,0:T(8,128)(2,1)S(1)}, u32[]{:S(2)}, u32[]{:S(2)}) %collective-permute-start.16) | collective-permute-done | bytes 114720 | tf_op jit(solution)/shard_map/ppermute | solution.py:232
  55.7 0.7 %add_convert_fusion = bf16[8,7168]{1,0:T(8,128)(2,1)} fusion(bf16[8,7168]{1,0:T(8,128)(2,1)S(1)} %collective-permute-done.19, bf16[8,7168]{1,0:T(8,128)(2,1)S(1)} %collective-permute-done.18, bf16[8,7168]{1,0:T(8,128)(2,1)S(1)} %collective-permute-done.16, bf16[8,7168]{1,0:T(8,128)(2,1)S(1)} %collective-permute-done.13, ...), kind=kLoop, calls=%fused_computation.26 | loop fusion | flops 802816 | bytes 802816 | tf_op jit(solution)/shard_map/convert_element_type | solution.py:284
  (54 shorter events, 5.5 us)
Async XLA Ops:
  1.0 11.6 %collective-permute-start = (bf16[8,7296]{1,0:T(8,128)(2,1)S(1)}, bf16[8,7296]{1,0:T(8,128)(2,1)S(1)}, u32[]{:S(2)}, u32[]{:S(2)}) collective-permute-start(bf16[8,7296]{1,0:T(8,128)(2,1)S(1)} %shard_map.73), channel_id=1, source_target_pairs={{0,12},{4,8},{8,4},{12,0},{1,13},{5,9},{9,5},{13,1},{2,14},{6,10},... | collective-permute-start | bytes 350216 | tf_op jit(solution)/shard_map/ppermute | solution.py:232
  6.1 9.9 %collective-permute-start.3 = (bf16[8,7296]{1,0:T(8,128)(2,1)S(1)}, bf16[8,7296]{1,0:T(8,128)(2,1)S(1)}, u32[]{:S(2)}, u32[]{:S(2)}) collective-permute-start(bf16[8,7296]{1,0:T(8,128)(2,1)S(1)} %shard_map.73), channel_id=1, source_target_pairs={{0,8},{4,12},{8,0},{12,4},{1,9},{5,13},{9,1},{13,5},{2,10},{6,14},... | collective-permute-start | bytes 350216 | tf_op jit(solution)/shard_map/ppermute | solution.py:232
  6.1 11.5 %collective-permute-start.2 = (bf16[8,7296]{1,0:T(8,128)(2,1)S(1)}, bf16[8,7296]{1,0:T(8,128)(2,1)S(1)}, u32[]{:S(2)}, u32[]{:S(2)}) collective-permute-start(bf16[8,7296]{1,0:T(8,128)(2,1)S(1)} %shard_map.73), channel_id=1, source_target_pairs={{0,6},{1,7},{2,4},{3,5},{4,2},{5,3},{6,0},{7,1},{8,14},{9,15},{10,... | collective-permute-start | bytes 350216 | tf_op jit(solution)/shard_map/ppermute | solution.py:246
  7.8 12.9 %collective-permute-start.1 = (bf16[8,7296]{1,0:T(8,128)(2,1)S(1)}, bf16[8,7296]{1,0:T(8,128)(2,1)S(1)}, u32[]{:S(2)}, u32[]{:S(2)}) collective-permute-start(bf16[8,7296]{1,0:T(8,128)(2,1)S(1)} %shard_map.73), channel_id=1, source_target_pairs={{0,2},{1,3},{2,0},{3,1},{4,6},{5,7},{6,4},{7,5},{8,10},{9,11},{10,... | collective-permute-start | bytes 350216 | tf_op jit(solution)/shard_map/ppermute | solution.py:233
  8.2 12.7 %collective-permute-start.6 = (bf16[8,7296]{1,0:T(8,128)(2,1)S(1)}, bf16[8,7296]{1,0:T(8,128)(2,1)S(1)}, u32[]{:S(2)}, u32[]{:S(2)}) collective-permute-start(bf16[8,7296]{1,0:T(8,128)(2,1)S(1)} %shard_map.73), channel_id=1, source_target_pairs={{0,4},{4,0},{8,12},{12,8},{1,5},{5,1},{9,13},{13,9},{2,6},{6,2},{1... | collective-permute-start | bytes 350216 | tf_op jit(solution)/shard_map/ppermute | solution.py:232
  9.6 2.6 %copy-start = (f32[1,56,16]{1,2,0:T(8,128)S(1)}, f32[1,56,16]{1,2,0:T(8,128)}, u32[]{:S(2)}) copy-start(f32[1,56,16]{1,2,0:T(8,128)} %param.11) | copy-start | bytes 10756
  9.6 2.6 %copy-start.1 = (f32[1,8,56]{2,1,0:T(8,128)S(1)}, f32[1,8,56]{2,1,0:T(8,128)}, u32[]{:S(2)}) copy-start(f32[1,8,56]{2,1,0:T(8,128)} %param.13) | copy-start | bytes 5380
  12.5 8.1 %collective-permute-start.5 = (bf16[8,7296]{1,0:T(8,128)(2,1)S(1)}, bf16[8,7296]{1,0:T(8,128)(2,1)S(1)}, u32[]{:S(2)}, u32[]{:S(2)}) collective-permute-start(bf16[8,7296]{1,0:T(8,128)(2,1)S(1)} %collective-permute-done), channel_id=1, source_target_pairs={{0,2},{1,3},{2,0},{3,1},{4,6},{5,7},{6,4},{7,5},{8,10},{9,11},{10,... | collective-permute-start | bytes 350216 | tf_op jit(solution)/shard_map/ppermute | solution.py:233
  16.0 4.8 %collective-permute-start.4 = (bf16[8,7296]{1,0:T(8,128)(2,1)S(1)}, bf16[8,7296]{1,0:T(8,128)(2,1)S(1)}, u32[]{:S(2)}, u32[]{:S(2)}) collective-permute-start(bf16[8,7296]{1,0:T(8,128)(2,1)S(1)} %collective-permute-done.3), channel_id=1, source_target_pairs={{0,2},{1,3},{2,0},{3,1},{4,6},{5,7},{6,4},{7,5},{8,10},{9,11},{10,... | collective-permute-start | bytes 350216 | tf_op jit(solution)/shard_map/ppermute | solution.py:233
  21.0 1.6 %collective-permute-start.7 = (bf16[16,7296]{1,0:T(8,128)(2,1)S(1)}, bf16[16,7296]{1,0:T(8,128)(2,1)S(1)}, u32[]{:S(2)}, u32[]{:S(2)}) collective-permute-start(bf16[16,7296]{1,0:T(8,128)(2,1)S(1)} %pad_maximum_fusion), channel_id=1, source_target_pairs={{0,1},{1,0},{2,3},{3,2},{4,5},{5,4},{6,7},{7,6},{8,9},{9,8},{10,11... | collective-permute-start | bytes 700424 | tf_op jit(solution)/shard_map/ppermute | solution.py:233
  21.1 1.8 %collective-permute-start.8 = (bf16[16,7296]{1,0:T(8,128)(2,1)S(1)}, bf16[16,7296]{1,0:T(8,128)(2,1)S(1)}, u32[]{:S(2)}, u32[]{:S(2)}) collective-permute-start(bf16[16,7296]{1,0:T(8,128)(2,1)S(1)} %pad_maximum_fusion.1), channel_id=1, source_target_pairs={{0,1},{1,0},{2,3},{3,2},{4,5},{5,4},{6,7},{7,6},{8,9},{9,8},{10,11... | collective-permute-start | bytes 700424 | tf_op jit(solution)/shard_map/ppermute | solution.py:233
  21.7 1.6 %collective-permute-start.9 = (bf16[16,7296]{1,0:T(8,128)(2,1)S(1)}, bf16[16,7296]{1,0:T(8,128)(2,1)S(1)}, u32[]{:S(2)}, u32[]{:S(2)}) collective-permute-start(bf16[16,7296]{1,0:T(8,128)(2,1)S(1)} %pad_maximum_fusion.2), channel_id=1, source_target_pairs={{0,1},{1,0},{2,3},{3,2},{4,5},{5,4},{6,7},{7,6},{8,9},{9,8},{10,11... | collective-permute-start | bytes 700424 | tf_op jit(solution)/shard_map/ppermute | solution.py:233
  21.8 1.8 %collective-permute-start.10 = (bf16[16,7296]{1,0:T(8,128)(2,1)S(1)}, bf16[16,7296]{1,0:T(8,128)(2,1)S(1)}, u32[]{:S(2)}, u32[]{:S(2)}) collective-permute-start(bf16[16,7296]{1,0:T(8,128)(2,1)S(1)} %pad_maximum_fusion.3), channel_id=1, source_target_pairs={{0,1},{1,0},{2,3},{3,2},{4,5},{5,4},{6,7},{7,6},{8,9},{9,8},{10,11... | collective-permute-start | bytes 700424 | tf_op jit(solution)/shard_map/ppermute | solution.py:233
  34.5 1.6 %collective-permute-start.11 = (bf16[2,8,7168]{2,1,0:T(8,128)(2,1)S(1)}, bf16[2,8,7168]{2,1,0:T(8,128)(2,1)S(1)}, u32[]{:S(2)}, u32[]{:S(2)}) collective-permute-start(bf16[2,8,7168]{2,1,0:T(8,128)(2,1)S(1)} %get-tuple-element.34), channel_id=1, source_target_pairs={{0,1},{1,0},{2,3},{3,2},{4,5},{5,4},{6,7},{7,6},{8,9},{9,8},{10,11... | collective-permute-start | bytes 688136 | tf_op jit(solution)/shard_map/ppermute | solution.py:233
  34.8 1.6 %collective-permute-start.14 = (bf16[2,8,7168]{2,1,0:T(8,128)(2,1)S(1)}, bf16[2,8,7168]{2,1,0:T(8,128)(2,1)S(1)}, u32[]{:S(2)}, u32[]{:S(2)}) collective-permute-start(bf16[2,8,7168]{2,1,0:T(8,128)(2,1)S(1)} %get-tuple-element.33), channel_id=1, source_target_pairs={{0,1},{1,0},{2,3},{3,2},{4,5},{5,4},{6,7},{7,6},{8,9},{9,8},{10,11... | collective-permute-start | bytes 688136 | tf_op jit(solution)/shard_map/ppermute | solution.py:233
  35.1 1.6 %collective-permute-start.17 = (bf16[2,8,7168]{2,1,0:T(8,128)(2,1)S(1)}, bf16[2,8,7168]{2,1,0:T(8,128)(2,1)S(1)}, u32[]{:S(2)}, u32[]{:S(2)}) collective-permute-start(bf16[2,8,7168]{2,1,0:T(8,128)(2,1)S(1)} %get-tuple-element.32), channel_id=1, source_target_pairs={{0,1},{1,0},{2,3},{3,2},{4,5},{5,4},{6,7},{7,6},{8,9},{9,8},{10,11... | collective-permute-start | bytes 688136 | tf_op jit(solution)/shard_map/ppermute | solution.py:233
  35.3 1.7 %collective-permute-start.20 = (bf16[2,8,7168]{2,1,0:T(8,128)(2,1)S(1)}, bf16[2,8,7168]{2,1,0:T(8,128)(2,1)S(1)}, u32[]{:S(2)}, u32[]{:S(2)}) collective-permute-start(bf16[2,8,7168]{2,1,0:T(8,128)(2,1)S(1)} %get-tuple-element.31), channel_id=1, source_target_pairs={{0,1},{1,0},{2,3},{3,2},{4,5},{5,4},{6,7},{7,6},{8,9},{9,8},{10,11... | collective-permute-start | bytes 688136 | tf_op jit(solution)/shard_map/ppermute | solution.py:233
  37.3 6.0 %collective-permute-start.12 = (bf16[8,7168]{1,0:T(8,128)(2,1)S(1)}, bf16[8,7168]{1,0:T(8,128)(2,1)S(1)}, u32[]{:S(2)}, u32[]{:S(2)}) collective-permute-start(bf16[8,7168]{1,0:T(8,128)(2,1)S(1)} %slice_bitcast_fusion.14), channel_id=1, source_target_pairs={{0,2},{1,3},{2,0},{3,1},{4,6},{5,7},{6,4},{7,5},{8,10},{9,11},{10,... | collective-permute-start | bytes 344072 | tf_op jit(solution)/shard_map/ppermute | solution.py:233
  38.8 9.4 %collective-permute-start.15 = (bf16[8,7168]{1,0:T(8,128)(2,1)S(1)}, bf16[8,7168]{1,0:T(8,128)(2,1)S(1)}, u32[]{:S(2)}, u32[]{:S(2)}) collective-permute-start(bf16[8,7168]{1,0:T(8,128)(2,1)S(1)} %slice_bitcast_fusion.12), channel_id=1, source_target_pairs={{0,2},{1,3},{2,0},{3,1},{4,6},{5,7},{6,4},{7,5},{8,10},{9,11},{10,... | collective-permute-start | bytes 344072 | tf_op jit(solution)/shard_map/ppermute | solution.py:233
  39.5 10.3 %collective-permute-start.18 = (bf16[8,7168]{1,0:T(8,128)(2,1)S(1)}, bf16[8,7168]{1,0:T(8,128)(2,1)S(1)}, u32[]{:S(2)}, u32[]{:S(2)}) collective-permute-start(bf16[8,7168]{1,0:T(8,128)(2,1)S(1)} %get-tuple-element.35), channel_id=1, source_target_pairs={{0,4},{1,5},{2,6},{3,7},{4,0},{5,1},{6,2},{7,3},{8,12},{9,13},{10,... | collective-permute-start | bytes 344072 | tf_op jit(solution)/shard_map/ppermute | solution.py:246
  40.7 9.1 %collective-permute-start.19 = (bf16[8,7168]{1,0:T(8,128)(2,1)S(1)}, bf16[8,7168]{1,0:T(8,128)(2,1)S(1)}, u32[]{:S(2)}, u32[]{:S(2)}) collective-permute-start(bf16[8,7168]{1,0:T(8,128)(2,1)S(1)} %get-tuple-element.36), channel_id=1, source_target_pairs={{0,6},{1,7},{2,4},{3,5},{4,2},{5,3},{6,0},{7,1},{8,14},{9,15},{10,... | collective-permute-start | bytes 344072 | tf_op jit(solution)/shard_map/ppermute | solution.py:246
  42.5 7.5 %collective-permute-start.21 = (bf16[8,7168]{1,0:T(8,128)(2,1)S(1)}, bf16[8,7168]{1,0:T(8,128)(2,1)S(1)}, u32[]{:S(2)}, u32[]{:S(2)}) collective-permute-start(bf16[8,7168]{1,0:T(8,128)(2,1)S(1)} %slice_bitcast_fusion.8), channel_id=1, source_target_pairs={{0,2},{1,3},{2,0},{3,1},{4,6},{5,7},{6,4},{7,5},{8,10},{9,11},{10,... | collective-permute-start | bytes 344072 | tf_op jit(solution)/shard_map/ppermute | solution.py:233
  43.3 7.4 %collective-permute-start.13 = (bf16[8,7168]{1,0:T(8,128)(2,1)S(1)}, bf16[8,7168]{1,0:T(8,128)(2,1)S(1)}, u32[]{:S(2)}, u32[]{:S(2)}) collective-permute-start(bf16[8,7168]{1,0:T(8,128)(2,1)S(1)} %fusion.6), channel_id=1, source_target_pairs={{0,12},{4,8},{8,4},{12,0},{1,13},{5,9},{9,5},{13,1},{2,14},{6,10},... | collective-permute-start | bytes 344072 | tf_op jit(solution)/shard_map/ppermute | solution.py:232
  48.3 7.5 %collective-permute-start.16 = (bf16[8,7168]{1,0:T(8,128)(2,1)S(1)}, bf16[8,7168]{1,0:T(8,128)(2,1)S(1)}, u32[]{:S(2)}, u32[]{:S(2)}) collective-permute-start(bf16[8,7168]{1,0:T(8,128)(2,1)S(1)} %fusion.5), channel_id=1, source_target_pairs={{0,8},{4,12},{8,0},{12,4},{1,9},{5,13},{9,1},{13,5},{2,10},{6,14},... | collective-permute-start | bytes 344072 | tf_op jit(solution)/shard_map/ppermute | solution.py:232

commit v5 on v4

--- a/solution.py
+++ b/solution.py
@@ -275,7 +275,7 @@
         return total.astype(jnp.bfloat16)
 
     over_pieces = lambda v: [over_local(v[dx], 2 * dx) for dx in range(1, chip_count)]
-    far = range(node_count - 1, 1, -1)
+    far = range(2, node_count)
     arrived = {dz: over_pieces(sums[dz]) for dz in far}
     returned = [over_node(group_sum(sums[dz][0], arrived[dz]), dz) for dz in far]
     returned += [over_both(sums[1][dx], 1, dx) for dx in range(chip_count)]

time: 56.6 us -> 55.1 us (0.973)
  waiting for transfers between devices: 13.4 us -> 11.1 us
  starting transfers between devices: 23.7 us -> 24.4 us
    ppermute x5, waiting for transfers between devices: 7.66 us -> 5.79 us  [shards(): over_node = lambda v, d: lax.ppermute(v, 'node', xor_pairs(node_count, d))]
    ppermute x5, starting transfers between devices: 10.5 us -> 11.2 us  [shards(): over_node = lambda v, d: lax.ppermute(v, 'node', xor_pairs(node_count, d))]
  transfers between devices with their start and end apart: 22 -> 22, of which waited for: 15 -> 13; matrix products, arithmetic and copies ran while one was open for 0% -> 0% of each run, Pallas kernels for 11% -> 11%
where the time goes in v5:
time: 55.1 us; the launch traced here: 54.9 us
  starting transfers between devices  24.4 us (44%)
  Pallas kernels  17.7 us (32%)
  waiting for transfers between devices  11.1 us (20%)
  other arithmetic  1.08 us (2%)
    ppermute x5, starting transfers between devices, shards(): over_node = lambda v, d: lax.ppermute(v, 'node', xor_pairs(node_count, d))  11.2 us
    pallas_call x1, Pallas kernels, expert_apply(): pl.pallas_call(functools.partial(expert_kernel, slice_count, pieces), out...  10.8 us
    ppermute x14, starting transfers between devices, shards(): lax.ppermute(v, 'local', xor_pairs(local_count, d))  8.48 us
    ppermute x5, waiting for transfers between devices, shards(): over_node = lambda v, d: lax.ppermute(v, 'node', xor_pairs(node_count, d))  5.79 us
    pallas_call x2, Pallas kernels, load_rows(): pl.pallas_call(functools.partial(load_kernel, start), out_shape=pltpu.VME...  5.69 us
    ppermute x14, waiting for transfers between devices, shards(): lax.ppermute(v, 'local', xor_pairs(local_count, d))  5.35 us
    ppermute x3, starting transfers between devices, shards(): lax.ppermute(v, ('node', 'local'), xor_pairs(node_count * local_count, dz...  4.73 us
  transfers between devices with their start and end apart: 22, of which 13 were waited for; matrix products, arithmetic and copies ran while one was open for 0% of the time, Pallas kernels for 11%

profile of v5, /device:TPU:0, one launch (start us, length us, event | category | flops | bytes accessed | tf_op | source)
XLA Modules:
  0.0 54.9 jit_solution(11860398482673991349)
XLA Ops:
  0.0 1.0 %shard_map.73 = bf16[8,7296]{1,0:T(8,128)(2,1)S(1)} custom-call(bf16[8,7168]{1,0:T(8,128)(2,1)} %tokens_hbm.1, s32[8,8]{1,0:T(8,128)} %ids_hbm.1, bf16[8,8]{1,0:T(8,128)(2,1)} %gates_hbm.1), custom_call_target="tpu_custom_call" | custom-call | tf_op jit(solution)/shard_map/pallas_call | solution.py:41
  1.0 5.1 %collective-permute-start = (bf16[8,7296]{1,0:T(8,128)(2,1)S(1)}, bf16[8,7296]{1,0:T(8,128)(2,1)S(1)}, u32[]{:S(2)}, u32[]{:S(2)}) collective-permute-start(bf16[8,7296]{1,0:T(8,128)(2,1)S(1)} %shard_map.73), channel_id=1, source_target_pairs={{0,12},{4,8},{8,4},{12,0},{1,13},{5,9},{9,5},{13,1},{2,14},{6,10},... | collective-permute-start | bytes 350216 | tf_op jit(solution)/shard_map/ppermute | solution.py:232
  6.1 1.7 %collective-permute-start.2 = (bf16[8,7296]{1,0:T(8,128)(2,1)S(1)}, bf16[8,7296]{1,0:T(8,128)(2,1)S(1)}, u32[]{:S(2)}, u32[]{:S(2)}) collective-permute-start(bf16[8,7296]{1,0:T(8,128)(2,1)S(1)} %shard_map.73), channel_id=1, source_target_pairs={{0,6},{1,7},{2,4},{3,5},{4,2},{5,3},{6,0},{7,1},{8,14},{9,15},{10,... | collective-permute-start | bytes 350216 | tf_op jit(solution)/shard_map/ppermute | solution.py:246
  7.8 0.4 collective-permute-start.1
  8.2 1.4 %collective-permute-start.6 = (bf16[8,7296]{1,0:T(8,128)(2,1)S(1)}, bf16[8,7296]{1,0:T(8,128)(2,1)S(1)}, u32[]{:S(2)}, u32[]{:S(2)}) collective-permute-start(bf16[8,7296]{1,0:T(8,128)(2,1)S(1)} %shard_map.73), channel_id=1, source_target_pairs={{0,4},{4,0},{8,12},{12,8},{1,5},{5,1},{9,13},{13,9},{2,6},{6,2},{1... | collective-permute-start | bytes 350216 | tf_op jit(solution)/shard_map/ppermute | solution.py:232
  9.6 2.6 %shard_map.74.refs_0_ = bf16[2688,1024]{1,0:T(8,128)(2,1)S(1)} custom-call(bf16[7168,2048]{1,0:T(8,128)(2,1)} %bitcast.64), custom_call_target="tpu_custom_call" | custom-call | bytes 5505024 | tf_op jit(solution)/shard_map/pallas_call | solution.py:101
  12.5 1.6 %collective-permute-start.5 = (bf16[8,7296]{1,0:T(8,128)(2,1)S(1)}, bf16[8,7296]{1,0:T(8,128)(2,1)S(1)}, u32[]{:S(2)}, u32[]{:S(2)}) collective-permute-start(bf16[8,7296]{1,0:T(8,128)(2,1)S(1)} %collective-permute-done), channel_id=1, source_target_pairs={{0,2},{1,3},{2,0},{3,1},{4,6},{5,7},{6,4},{7,5},{8,10},{9,11},{10,... | collective-permute-start | bytes 350216 | tf_op jit(solution)/shard_map/ppermute | solution.py:233
  14.1 1.9 %collective-permute-done.3 = bf16[8,7296]{1,0:T(8,128)(2,1)S(1)} collective-permute-done((bf16[8,7296]{1,0:T(8,128)(2,1)S(1)}, bf16[8,7296]{1,0:T(8,128)(2,1)S(1)}, u32[]{:S(2)}, u32[]{:S(2)}) %collective-permute-start.3) | collective-permute-done | bytes 116768 | tf_op jit(solution)/shard_map/ppermute | solution.py:232
  16.0 1.5 %collective-permute-start.4 = (bf16[8,7296]{1,0:T(8,128)(2,1)S(1)}, bf16[8,7296]{1,0:T(8,128)(2,1)S(1)}, u32[]{:S(2)}, u32[]{:S(2)}) collective-permute-start(bf16[8,7296]{1,0:T(8,128)(2,1)S(1)} %collective-permute-done.3), channel_id=1, source_target_pairs={{0,2},{1,3},{2,0},{3,1},{4,6},{5,7},{6,4},{7,5},{8,10},{9,11},{10,... | collective-permute-start | bytes 350216 | tf_op jit(solution)/shard_map/ppermute | solution.py:233
  17.5 3.1 %shard_map.75.refs_1_ = bf16[3584,1024]{1,0:T(8,128)(2,1)S(1)} custom-call(bf16[7168,2048]{1,0:T(8,128)(2,1)} %bitcast.65), custom_call_target="tpu_custom_call" | custom-call | bytes 7340032 | tf_op jit(solution)/shard_map/pallas_call | solution.py:101
  21.1 0.6 %collective-permute-start.8 = (bf16[16,7296]{1,0:T(8,128)(2,1)S(1)}, bf16[16,7296]{1,0:T(8,128)(2,1)S(1)}, u32[]{:S(2)}, u32[]{:S(2)}) collective-permute-start(bf16[16,7296]{1,0:T(8,128)(2,1)S(1)} %pad_maximum_fusion.1), channel_id=1, source_target_pairs={{0,1},{1,0},{2,3},{3,2},{4,5},{5,4},{6,7},{7,6},{8,9},{9,8},{10,11... | collective-permute-start | bytes 700424 | tf_op jit(solution)/shard_map/ppermute | solution.py:233
  21.8 0.5 collective-permute-start.10
  23.6 10.8 %shard_map.77 = bf16[128,7168]{1,0:T(8,128)(2,1)S(1)} custom-call(bf16[128,7296]{1,0:T(8,128)(2,1)S(1)} %constant_dynamic-update-slice_fusion.rows_ref, bf16[2688,1024]{1,0:T(8,128)(2,1)S(1)} %shard_map.74.refs_0_, bf16[3584,1024]{1,0:T(8,128)(2,1)S(1)} %shard_map.75.refs_1_, bf16[56,2048]{1,0:T(8,128)(2,1)S(1)} %get-tuple-element.25.refs_2_, ...), custom_call_target="tpu_custom_call" | custom-call | flops 5637144576 | bytes 22020096 | tf_op jit(solution)/shard_map/pallas_call | solution.py:190
  35.6 0.5 collective-permute-done.11
  37.3 1.6 %collective-permute-start.12 = (bf16[8,7168]{1,0:T(8,128)(2,1)S(1)}, bf16[8,7168]{1,0:T(8,128)(2,1)S(1)}, u32[]{:S(2)}, u32[]{:S(2)}) collective-permute-start(bf16[8,7168]{1,0:T(8,128)(2,1)S(1)} %slice_bitcast_fusion.14), channel_id=1, source_target_pairs={{0,2},{1,3},{2,0},{3,1},{4,6},{5,7},{6,4},{7,5},{8,10},{9,11},{10,... | collective-permute-start | bytes 344072 | tf_op jit(solution)/shard_map/ppermute | solution.py:233
  38.8 0.6 %collective-permute-start.15 = (bf16[8,7168]{1,0:T(8,128)(2,1)S(1)}, bf16[8,7168]{1,0:T(8,128)(2,1)S(1)}, u32[]{:S(2)}, u32[]{:S(2)}) collective-permute-start(bf16[8,7168]{1,0:T(8,128)(2,1)S(1)} %slice_bitcast_fusion.12), channel_id=1, source_target_pairs={{0,2},{1,3},{2,0},{3,1},{4,6},{5,7},{6,4},{7,5},{8,10},{9,11},{10,... | collective-permute-start | bytes 344072 | tf_op jit(solution)/shard_map/ppermute | solution.py:233
  39.5 1.2 %collective-permute-start.18 = (bf16[8,7168]{1,0:T(8,128)(2,1)S(1)}, bf16[8,7168]{1,0:T(8,128)(2,1)S(1)}, u32[]{:S(2)}, u32[]{:S(2)}) collective-permute-start(bf16[8,7168]{1,0:T(8,128)(2,1)S(1)} %get-tuple-element.35), channel_id=1, source_target_pairs={{0,4},{1,5},{2,6},{3,7},{4,0},{5,1},{6,2},{7,3},{8,12},{9,13},{10,... | collective-permute-start | bytes 344072 | tf_op jit(solution)/shard_map/ppermute | solution.py:246
  40.7 1.8 %collective-permute-start.19 = (bf16[8,7168]{1,0:T(8,128)(2,1)S(1)}, bf16[8,7168]{1,0:T(8,128)(2,1)S(1)}, u32[]{:S(2)}, u32[]{:S(2)}) collective-permute-start(bf16[8,7168]{1,0:T(8,128)(2,1)S(1)} %get-tuple-element.36), channel_id=1, source_target_pairs={{0,6},{1,7},{2,4},{3,5},{4,2},{5,3},{6,0},{7,1},{8,14},{9,15},{10,... | collective-permute-start | bytes 344072 | tf_op jit(solution)/shard_map/ppermute | solution.py:246
  42.5 0.6 %collective-permute-start.21 = (bf16[8,7168]{1,0:T(8,128)(2,1)S(1)}, bf16[8,7168]{1,0:T(8,128)(2,1)S(1)}, u32[]{:S(2)}, u32[]{:S(2)}) collective-permute-start(bf16[8,7168]{1,0:T(8,128)(2,1)S(1)} %slice_bitcast_fusion.8), channel_id=1, source_target_pairs={{0,2},{1,3},{2,0},{3,1},{4,6},{5,7},{6,4},{7,5},{8,10},{9,11},{10,... | collective-permute-start | bytes 344072 | tf_op jit(solution)/shard_map/ppermute | solution.py:233
  43.3 1.7 %collective-permute-start.13 = (bf16[8,7168]{1,0:T(8,128)(2,1)S(1)}, bf16[8,7168]{1,0:T(8,128)(2,1)S(1)}, u32[]{:S(2)}, u32[]{:S(2)}) collective-permute-start(bf16[8,7168]{1,0:T(8,128)(2,1)S(1)} %fusion.6), channel_id=1, source_target_pairs={{0,8},{4,12},{8,0},{12,4},{1,9},{5,13},{9,1},{13,5},{2,10},{6,14},... | collective-permute-start | bytes 344072 | tf_op jit(solution)/shard_map/ppermute | solution.py:232
  45.0 2.2 %collective-permute-done.15 = bf16[8,7168]{1,0:T(8,128)(2,1)S(1)} collective-permute-done((bf16[8,7168]{1,0:T(8,128)(2,1)S(1)}, bf16[8,7168]{1,0:T(8,128)(2,1)S(1)}, u32[]{:S(2)}, u32[]{:S(2)}) %collective-permute-start.15) | collective-permute-done | bytes 114720 | tf_op jit(solution)/shard_map/ppermute | solution.py:233
  47.3 3.0 %collective-permute-start.16 = (bf16[8,7168]{1,0:T(8,128)(2,1)S(1)}, bf16[8,7168]{1,0:T(8,128)(2,1)S(1)}, u32[]{:S(2)}, u32[]{:S(2)}) collective-permute-start(bf16[8,7168]{1,0:T(8,128)(2,1)S(1)} %fusion.5), channel_id=1, source_target_pairs={{0,12},{4,8},{8,4},{12,0},{1,13},{5,9},{9,5},{13,1},{2,14},{6,10},... | collective-permute-start | bytes 344072 | tf_op jit(solution)/shard_map/ppermute | solution.py:232
  50.3 3.8 %collective-permute-done.13 = bf16[8,7168]{1,0:T(8,128)(2,1)S(1)} collective-permute-done((bf16[8,7168]{1,0:T(8,128)(2,1)S(1)}, bf16[8,7168]{1,0:T(8,128)(2,1)S(1)}, u32[]{:S(2)}, u32[]{:S(2)}) %collective-permute-start.13) | collective-permute-done | bytes 114720 | tf_op jit(solution)/shard_map/ppermute | solution.py:232
  54.1 0.7 %add_convert_fusion = bf16[8,7168]{1,0:T(8,128)(2,1)} fusion(bf16[8,7168]{1,0:T(8,128)(2,1)S(1)} %collective-permute-done.19, bf16[8,7168]{1,0:T(8,128)(2,1)S(1)} %collective-permute-done.18, bf16[8,7168]{1,0:T(8,128)(2,1)S(1)} %collective-permute-done.16, bf16[8,7168]{1,0:T(8,128)(2,1)S(1)} %collective-permute-done.13, ...), kind=kLoop, calls=%fused_computation.26 | loop fusion | flops 802816 | bytes 802816 | tf_op jit(solution)/shard_map/convert_element_type | solution.py:284
  (54 shorter events, 4.9 us)
Async XLA Ops:
  1.0 11.6 %collective-permute-start = (bf16[8,7296]{1,0:T(8,128)(2,1)S(1)}, bf16[8,7296]{1,0:T(8,128)(2,1)S(1)}, u32[]{:S(2)}, u32[]{:S(2)}) collective-permute-start(bf16[8,7296]{1,0:T(8,128)(2,1)S(1)} %shard_map.73), channel_id=1, source_target_pairs={{0,12},{4,8},{8,4},{12,0},{1,13},{5,9},{9,5},{13,1},{2,14},{6,10},... | collective-permute-start | bytes 350216 | tf_op jit(solution)/shard_map/ppermute | solution.py:232
  6.1 9.9 %collective-permute-start.3 = (bf16[8,7296]{1,0:T(8,128)(2,1)S(1)}, bf16[8,7296]{1,0:T(8,128)(2,1)S(1)}, u32[]{:S(2)}, u32[]{:S(2)}) collective-permute-start(bf16[8,7296]{1,0:T(8,128)(2,1)S(1)} %shard_map.73), channel_id=1, source_target_pairs={{0,8},{4,12},{8,0},{12,4},{1,9},{5,13},{9,1},{13,5},{2,10},{6,14},... | collective-permute-start | bytes 350216 | tf_op jit(solution)/shard_map/ppermute | solution.py:232
  6.1 11.5 %collective-permute-start.2 = (bf16[8,7296]{1,0:T(8,128)(2,1)S(1)}, bf16[8,7296]{1,0:T(8,128)(2,1)S(1)}, u32[]{:S(2)}, u32[]{:S(2)}) collective-permute-start(bf16[8,7296]{1,0:T(8,128)(2,1)S(1)} %shard_map.73), channel_id=1, source_target_pairs={{0,6},{1,7},{2,4},{3,5},{4,2},{5,3},{6,0},{7,1},{8,14},{9,15},{10,... | collective-permute-start | bytes 350216 | tf_op jit(solution)/shard_map/ppermute | solution.py:246
  7.8 12.9 %collective-permute-start.1 = (bf16[8,7296]{1,0:T(8,128)(2,1)S(1)}, bf16[8,7296]{1,0:T(8,128)(2,1)S(1)}, u32[]{:S(2)}, u32[]{:S(2)}) collective-permute-start(bf16[8,7296]{1,0:T(8,128)(2,1)S(1)} %shard_map.73), channel_id=1, source_target_pairs={{0,2},{1,3},{2,0},{3,1},{4,6},{5,7},{6,4},{7,5},{8,10},{9,11},{10,... | collective-permute-start | bytes 350216 | tf_op jit(solution)/shard_map/ppermute | solution.py:233
  8.2 12.7 %collective-permute-start.6 = (bf16[8,7296]{1,0:T(8,128)(2,1)S(1)}, bf16[8,7296]{1,0:T(8,128)(2,1)S(1)}, u32[]{:S(2)}, u32[]{:S(2)}) collective-permute-start(bf16[8,7296]{1,0:T(8,128)(2,1)S(1)} %shard_map.73), channel_id=1, source_target_pairs={{0,4},{4,0},{8,12},{12,8},{1,5},{5,1},{9,13},{13,9},{2,6},{6,2},{1... | collective-permute-start | bytes 350216 | tf_op jit(solution)/shard_map/ppermute | solution.py:232
  9.6 2.6 %copy-start = (f32[1,56,16]{1,2,0:T(8,128)S(1)}, f32[1,56,16]{1,2,0:T(8,128)}, u32[]{:S(2)}) copy-start(f32[1,56,16]{1,2,0:T(8,128)} %param.11) | copy-start | bytes 10756
  9.6 2.6 %copy-start.1 = (f32[1,8,56]{2,1,0:T(8,128)S(1)}, f32[1,8,56]{2,1,0:T(8,128)}, u32[]{:S(2)}) copy-start(f32[1,8,56]{2,1,0:T(8,128)} %param.13) | copy-start | bytes 5380
  12.5 8.1 %collective-permute-start.5 = (bf16[8,7296]{1,0:T(8,128)(2,1)S(1)}, bf16[8,7296]{1,0:T(8,128)(2,1)S(1)}, u32[]{:S(2)}, u32[]{:S(2)}) collective-permute-start(bf16[8,7296]{1,0:T(8,128)(2,1)S(1)} %collective-permute-done), channel_id=1, source_target_pairs={{0,2},{1,3},{2,0},{3,1},{4,6},{5,7},{6,4},{7,5},{8,10},{9,11},{10,... | collective-permute-start | bytes 350216 | tf_op jit(solution)/shard_map/ppermute | solution.py:233
  16.0 4.8 %collective-permute-start.4 = (bf16[8,7296]{1,0:T(8,128)(2,1)S(1)}, bf16[8,7296]{1,0:T(8,128)(2,1)S(1)}, u32[]{:S(2)}, u32[]{:S(2)}) collective-permute-start(bf16[8,7296]{1,0:T(8,128)(2,1)S(1)} %collective-permute-done.3), channel_id=1, source_target_pairs={{0,2},{1,3},{2,0},{3,1},{4,6},{5,7},{6,4},{7,5},{8,10},{9,11},{10,... | collective-permute-start | bytes 350216 | tf_op jit(solution)/shard_map/ppermute | solution.py:233
  21.0 1.6 %collective-permute-start.7 = (bf16[16,7296]{1,0:T(8,128)(2,1)S(1)}, bf16[16,7296]{1,0:T(8,128)(2,1)S(1)}, u32[]{:S(2)}, u32[]{:S(2)}) collective-permute-start(bf16[16,7296]{1,0:T(8,128)(2,1)S(1)} %pad_maximum_fusion), channel_id=1, source_target_pairs={{0,1},{1,0},{2,3},{3,2},{4,5},{5,4},{6,7},{7,6},{8,9},{9,8},{10,11... | collective-permute-start | bytes 700424 | tf_op jit(solution)/shard_map/ppermute | solution.py:233
  21.1 1.8 %collective-permute-start.8 = (bf16[16,7296]{1,0:T(8,128)(2,1)S(1)}, bf16[16,7296]{1,0:T(8,128)(2,1)S(1)}, u32[]{:S(2)}, u32[]{:S(2)}) collective-permute-start(bf16[16,7296]{1,0:T(8,128)(2,1)S(1)} %pad_maximum_fusion.1), channel_id=1, source_target_pairs={{0,1},{1,0},{2,3},{3,2},{4,5},{5,4},{6,7},{7,6},{8,9},{9,8},{10,11... | collective-permute-start | bytes 700424 | tf_op jit(solution)/shard_map/ppermute | solution.py:233
  21.7 1.6 %collective-permute-start.9 = (bf16[16,7296]{1,0:T(8,128)(2,1)S(1)}, bf16[16,7296]{1,0:T(8,128)(2,1)S(1)}, u32[]{:S(2)}, u32[]{:S(2)}) collective-permute-start(bf16[16,7296]{1,0:T(8,128)(2,1)S(1)} %pad_maximum_fusion.2), channel_id=1, source_target_pairs={{0,1},{1,0},{2,3},{3,2},{4,5},{5,4},{6,7},{7,6},{8,9},{9,8},{10,11... | collective-permute-start | bytes 700424 | tf_op jit(solution)/shard_map/ppermute | solution.py:233
  21.8 1.8 %collective-permute-start.10 = (bf16[16,7296]{1,0:T(8,128)(2,1)S(1)}, bf16[16,7296]{1,0:T(8,128)(2,1)S(1)}, u32[]{:S(2)}, u32[]{:S(2)}) collective-permute-start(bf16[16,7296]{1,0:T(8,128)(2,1)S(1)} %pad_maximum_fusion.3), channel_id=1, source_target_pairs={{0,1},{1,0},{2,3},{3,2},{4,5},{5,4},{6,7},{7,6},{8,9},{9,8},{10,11... | collective-permute-start | bytes 700424 | tf_op jit(solution)/shard_map/ppermute | solution.py:233
  34.5 1.6 %collective-permute-start.11 = (bf16[2,8,7168]{2,1,0:T(8,128)(2,1)S(1)}, bf16[2,8,7168]{2,1,0:T(8,128)(2,1)S(1)}, u32[]{:S(2)}, u32[]{:S(2)}) collective-permute-start(bf16[2,8,7168]{2,1,0:T(8,128)(2,1)S(1)} %get-tuple-element.34), channel_id=1, source_target_pairs={{0,1},{1,0},{2,3},{3,2},{4,5},{5,4},{6,7},{7,6},{8,9},{9,8},{10,11... | collective-permute-start | bytes 688136 | tf_op jit(solution)/shard_map/ppermute | solution.py:233
  34.8 1.6 %collective-permute-start.14 = (bf16[2,8,7168]{2,1,0:T(8,128)(2,1)S(1)}, bf16[2,8,7168]{2,1,0:T(8,128)(2,1)S(1)}, u32[]{:S(2)}, u32[]{:S(2)}) collective-permute-start(bf16[2,8,7168]{2,1,0:T(8,128)(2,1)S(1)} %get-tuple-element.33), channel_id=1, source_target_pairs={{0,1},{1,0},{2,3},{3,2},{4,5},{5,4},{6,7},{7,6},{8,9},{9,8},{10,11... | collective-permute-start | bytes 688136 | tf_op jit(solution)/shard_map/ppermute | solution.py:233
  35.1 1.6 %collective-permute-start.17 = (bf16[2,8,7168]{2,1,0:T(8,128)(2,1)S(1)}, bf16[2,8,7168]{2,1,0:T(8,128)(2,1)S(1)}, u32[]{:S(2)}, u32[]{:S(2)}) collective-permute-start(bf16[2,8,7168]{2,1,0:T(8,128)(2,1)S(1)} %get-tuple-element.32), channel_id=1, source_target_pairs={{0,1},{1,0},{2,3},{3,2},{4,5},{5,4},{6,7},{7,6},{8,9},{9,8},{10,11... | collective-permute-start | bytes 688136 | tf_op jit(solution)/shard_map/ppermute | solution.py:233
  35.3 1.7 %collective-permute-start.20 = (bf16[2,8,7168]{2,1,0:T(8,128)(2,1)S(1)}, bf16[2,8,7168]{2,1,0:T(8,128)(2,1)S(1)}, u32[]{:S(2)}, u32[]{:S(2)}) collective-permute-start(bf16[2,8,7168]{2,1,0:T(8,128)(2,1)S(1)} %get-tuple-element.31), channel_id=1, source_target_pairs={{0,1},{1,0},{2,3},{3,2},{4,5},{5,4},{6,7},{7,6},{8,9},{9,8},{10,11... | collective-permute-start | bytes 688136 | tf_op jit(solution)/shard_map/ppermute | solution.py:233
  37.3 6.0 %collective-permute-start.12 = (bf16[8,7168]{1,0:T(8,128)(2,1)S(1)}, bf16[8,7168]{1,0:T(8,128)(2,1)S(1)}, u32[]{:S(2)}, u32[]{:S(2)}) collective-permute-start(bf16[8,7168]{1,0:T(8,128)(2,1)S(1)} %slice_bitcast_fusion.14), channel_id=1, source_target_pairs={{0,2},{1,3},{2,0},{3,1},{4,6},{5,7},{6,4},{7,5},{8,10},{9,11},{10,... | collective-permute-start | bytes 344072 | tf_op jit(solution)/shard_map/ppermute | solution.py:233
  38.8 8.4 %collective-permute-start.15 = (bf16[8,7168]{1,0:T(8,128)(2,1)S(1)}, bf16[8,7168]{1,0:T(8,128)(2,1)S(1)}, u32[]{:S(2)}, u32[]{:S(2)}) collective-permute-start(bf16[8,7168]{1,0:T(8,128)(2,1)S(1)} %slice_bitcast_fusion.12), channel_id=1, source_target_pairs={{0,2},{1,3},{2,0},{3,1},{4,6},{5,7},{6,4},{7,5},{8,10},{9,11},{10,... | collective-permute-start | bytes 344072 | tf_op jit(solution)/shard_map/ppermute | solution.py:233
  39.5 10.8 %collective-permute-start.18 = (bf16[8,7168]{1,0:T(8,128)(2,1)S(1)}, bf16[8,7168]{1,0:T(8,128)(2,1)S(1)}, u32[]{:S(2)}, u32[]{:S(2)}) collective-permute-start(bf16[8,7168]{1,0:T(8,128)(2,1)S(1)} %get-tuple-element.35), channel_id=1, source_target_pairs={{0,4},{1,5},{2,6},{3,7},{4,0},{5,1},{6,2},{7,3},{8,12},{9,13},{10,... | collective-permute-start | bytes 344072 | tf_op jit(solution)/shard_map/ppermute | solution.py:246
  40.7 9.6 %collective-permute-start.19 = (bf16[8,7168]{1,0:T(8,128)(2,1)S(1)}, bf16[8,7168]{1,0:T(8,128)(2,1)S(1)}, u32[]{:S(2)}, u32[]{:S(2)}) collective-permute-start(bf16[8,7168]{1,0:T(8,128)(2,1)S(1)} %get-tuple-element.36), channel_id=1, source_target_pairs={{0,6},{1,7},{2,4},{3,5},{4,2},{5,3},{6,0},{7,1},{8,14},{9,15},{10,... | collective-permute-start | bytes 344072 | tf_op jit(solution)/shard_map/ppermute | solution.py:246
  42.5 7.8 %collective-permute-start.21 = (bf16[8,7168]{1,0:T(8,128)(2,1)S(1)}, bf16[8,7168]{1,0:T(8,128)(2,1)S(1)}, u32[]{:S(2)}, u32[]{:S(2)}) collective-permute-start(bf16[8,7168]{1,0:T(8,128)(2,1)S(1)} %slice_bitcast_fusion.8), channel_id=1, source_target_pairs={{0,2},{1,3},{2,0},{3,1},{4,6},{5,7},{6,4},{7,5},{8,10},{9,11},{10,... | collective-permute-start | bytes 344072 | tf_op jit(solution)/shard_map/ppermute | solution.py:233
  43.3 10.8 %collective-permute-start.13 = (bf16[8,7168]{1,0:T(8,128)(2,1)S(1)}, bf16[8,7168]{1,0:T(8,128)(2,1)S(1)}, u32[]{:S(2)}, u32[]{:S(2)}) collective-permute-start(bf16[8,7168]{1,0:T(8,128)(2,1)S(1)} %fusion.6), channel_id=1, source_target_pairs={{0,8},{4,12},{8,0},{12,4},{1,9},{5,13},{9,1},{13,5},{2,10},{6,14},... | collective-permute-start | bytes 344072 | tf_op jit(solution)/shard_map/ppermute | solution.py:232
  47.3 6.8 %collective-permute-start.16 = (bf16[8,7168]{1,0:T(8,128)(2,1)S(1)}, bf16[8,7168]{1,0:T(8,128)(2,1)S(1)}, u32[]{:S(2)}, u32[]{:S(2)}) collective-permute-start(bf16[8,7168]{1,0:T(8,128)(2,1)S(1)} %fusion.5), channel_id=1, source_target_pairs={{0,12},{4,8},{8,4},{12,0},{1,13},{5,9},{9,5},{13,1},{2,14},{6,10},... | collective-permute-start | bytes 344072 | tf_op jit(solution)/shard_map/ppermute | solution.py:232
